TPU v7x, 32 devices: a whole 2x2x4 slice. The times are simulated.
32 devices in a mesh: hyp: 2 (over x), row: 4 (over z), col: 4 (over y, core).
Axes of the slice: x: 2, y: 2, z: 4, core: 2. Of those that a mesh axis runs over, the one named last changes fastest.
Arguments:
- sigma_root: bfloat16 [16384, 8192], P(('hyp', 'row'), 'col'), parts along dimension 0, as said below
- lower1: bfloat16 [16384, 2048], P(('hyp', 'row'), 'col'), parts along dimension 0, may hold values from -0.125 to 0.125
- mask1: int32 [32, 8], replicated, may hold values 0 or 1
- inv1: bfloat16 [16, 256, 256], P(('hyp', 'col')), parts along dimension 0
- lower2: bfloat16 [16384, 1024], P(('hyp', 'row'), 'col'), parts along dimension 0, may hold values from -0.125 to 0.125
- mask2: int32 [32, 4], replicated, may hold values 0 or 1
- link2: bfloat16 [8, 256, 256], P(('hyp', 'col')), parts along dimension 0, may hold values from -0.375 to 0.375
- inv2: bfloat16 [8, 256, 256], P(('hyp', 'col')), parts along dimension 0
- parent: int32 [4], replicated, may hold values from 0 to 7, as said below
Outputs:
- off1: bfloat16 [16384, 2048], P(('hyp', 'row'), 'col'), parts along dimension 0
- diag1: bfloat16 [16, 256, 256], P(('hyp', 'col')), parts along dimension 0
- off2: bfloat16 [16384, 1024], P(('hyp', 'row'), 'col'), parts along dimension 0
- par2: bfloat16 [8, 256, 256], P(('hyp', 'col')), parts along dimension 0
- diag2: bfloat16 [8, 256, 256], P(('hyp', 'col')), parts along dimension 0
There are 2 independent parts, one for each index of `hyp`. A program takes and returns all parts, laid end to end along the dimension named above; an argument that names none is the same for every part. Nothing has to cross between parts.
Inputs may be any that keep to these rules, and one draw needn't show every extreme that they name: `mask1`: 1 where block row i of the root lies in the structure of supernode p. `mask2`: 1 where block row i of the root lies in the structure of supernode k. The parent of supernode k lies in 2 * (k) to 2 * (k) + 1. `sigma_root`: symmetric.
All inputs are finite; a program needn't handle non-finite values.
Results may differ from a plain program's by a relative error of at most 0.0061.
Values may be sent and summed in bfloat16 or wider, within the bound.
A program may use at most 128 MiB of HBM per device.

v0:
```python
import jax
import jax.numpy as jnp
from jax import lax
from jax.sharding import PartitionSpec as P


def per_device(sigma_root, lower1, mask1, inv1, lower2, mask2, link2, inv2, parent):
    block = inv1.shape[1]
    rows = sigma_root.shape[0]
    row_blocks = rows // block
    count1 = inv1.shape[0]
    count2 = inv2.shape[0]
    row_id = lax.axis_index("row")
    col_id = lax.axis_index("col")

    def make_panel(lower, mask, inverse):
        count = inverse.shape[0]
        window = lax.dynamic_slice(mask, (row_id * row_blocks, col_id * count), (row_blocks, count))
        masked = (
            lower.reshape(row_blocks, block, count, block)
            * window.astype(jnp.bfloat16)[:, None, :, None]
        )
        masked = masked.reshape(rows, count, block)
        product = jnp.einsum("rpb,pbd->rpd", masked, inverse, preferred_element_type=jnp.float32)
        return product.astype(jnp.bfloat16).reshape(rows, count * block)

    panel1 = make_panel(lower1, mask1, inv1)
    panel2 = make_panel(lower2, mask2, inv2)
    root_rows = lax.all_gather(sigma_root, "col", axis=1, tiled=True)

    def root_product(panel):
        return jnp.dot(
            root_rows,
            lax.all_gather(panel, "row", axis=0, tiled=True),
            preferred_element_type=jnp.float32,
        )

    x_one = root_product(panel1)
    x_two = root_product(panel2)
    off1 = (-x_one).astype(jnp.bfloat16)
    off1_blocks = off1.reshape(rows, count1, block)
    term1 = jnp.einsum(
        "rpb,rpd->pbd",
        panel1.reshape(rows, count1, block),
        off1_blocks,
        preferred_element_type=jnp.float32,
    )
    term1 = lax.psum(term1, "row")
    base1 = jnp.einsum("pcb,pcd->pbd", inv1, inv1, preferred_element_type=jnp.float32)
    diag1 = (base1 - term1).astype(jnp.bfloat16)
    link_u = jnp.einsum("kbc,kcd->kbd", link2, inv2, preferred_element_type=jnp.float32).astype(
        jnp.bfloat16
    )
    local_parent = lax.dynamic_slice_in_dim(parent, col_id * count2, count2) - col_id * count1
    pick = (local_parent[:, None] == jnp.arange(count1, dtype=jnp.int32)[None, :]).astype(
        jnp.bfloat16
    )
    par_off = jnp.einsum(
        "kp,rpb->rkb", pick, off1_blocks, preferred_element_type=jnp.float32
    ).astype(jnp.bfloat16)
    par_diag = jnp.einsum("kp,pbd->kbd", pick, diag1, preferred_element_type=jnp.float32).astype(
        jnp.bfloat16
    )
    panel2_blocks = panel2.reshape(rows, count2, block)
    extra = jnp.einsum("rkb,kbd->rkd", par_off, link_u, preferred_element_type=jnp.float32)
    y_root = x_two + extra.reshape(rows, count2 * block)
    off2 = (-y_root).astype(jnp.bfloat16)
    cross = jnp.einsum("rkb,rkd->kbd", par_off, panel2_blocks, preferred_element_type=jnp.float32)
    pair = jnp.einsum(
        "rkb,rkd->kbd",
        panel2_blocks,
        off2.reshape(rows, count2, block),
        preferred_element_type=jnp.float32,
    )
    cross, pair = lax.psum((cross, pair), "row")
    y_par = cross + jnp.einsum("kbc,kcd->kbd", par_diag, link_u, preferred_element_type=jnp.float32)
    par2 = (-y_par).astype(jnp.bfloat16)
    base2 = jnp.einsum("kcb,kcd->kbd", inv2, inv2, preferred_element_type=jnp.float32)
    last = jnp.einsum("kcb,kcd->kbd", link_u, par2, preferred_element_type=jnp.float32)
    diag2 = (base2 - pair - last).astype(jnp.bfloat16)
    return (off1, diag1, off2, par2, diag2)


def solution(mesh):
    placed = (
        P(("hyp", "row"), "col"),
        P(("hyp", "row"), "col"),
        P(),
        P(("hyp", "col"), None, None),
        P(("hyp", "row"), "col"),
        P(),
        P(("hyp", "col"), None, None),
        P(("hyp", "col"), None, None),
        P(),
    )
    return jax.shard_map(
        per_device,
        mesh=mesh,
        in_specs=placed,
        out_specs=(
            P(("hyp", "row"), "col"),
            P(("hyp", "col"), None, None),
            P(("hyp", "row"), "col"),
            P(("hyp", "col"), None, None),
            P(("hyp", "col"), None, None),
        ),
        check_vma=False,
    )
```

profile of v0, /device:TPU:10, one launch (start us, length us, event | category | flops | bytes accessed | tf_op | source)
XLA Modules:
  0.0 529.8 jit_solution(16363809849330396391)
XLA Ops:
  7.2 0.8 dynamic-slice_convert_fusion
  8.0 0.1 broadcast_bitcast_fusion
  8.1 3.9 convolution_convert_fusion
  12.1 0.7 all-gather.6.cloned.1.call-update
  12.9 0.8 convert_bitcast_fusion
  13.7 0.1 broadcast_bitcast_fusion.1
  13.7 1.5 convolution_convert_fusion.1
  15.2 0.0 all-reduce.3.cloned.1.call-start
  15.3 0.6 dynamic_slice.11
  16.5 0.2 convolution_convert_fusion.2
  16.7 143.5 %all-gather.4.cloned.1.call-done = bf16[8192,512]{0,1:T(8,128)(2,1)} async-done(((bf16[2048,512]{0,1:T(8,128)(2,1)}), bf16[8192,512]{0,1:T(8,128)(2,1)}) %all-gather.4.cloned.1.call-update) | async-done | bytes 8388624 | tf_op jit(solution)/shard_map/all_gather | solution.py:34
  160.2 204.1 %all-gather.6.cloned.1.call-done = bf16[2048,8192]{1,0:T(8,128)(2,1)} async-done(((bf16[2048,2048]{1,0:T(8,128)(2,1)}), bf16[2048,8192]{1,0:T(8,128)(2,1)}) %all-gather.6.cloned.1.call-update) | async-done | bytes 33554448 | tf_op jit(solution)/shard_map/all_gather | solution.py:29
  364.3 23.9 %negate_convert_fusion = bf16[512,2048]{1,0:T(8,128)(2,1)S(1)} fusion(bf16[8192,512]{0,1:T(8,128)(2,1)} %all-gather.4.cloned.1.call-done, bf16[2048,8192]{1,0:T(8,128)(2,1)} %all-gather.6.cloned.1.call-done), kind=kOutput, calls=%fused_computation | convolution fusion | flops 17181966336 | bytes 44040192 | tf_op jit(solution)/shard_map/dot_general | solution.py:32
  388.2 3.8 copy.23
  392.0 4.0 fusion.23
  396.0 1.3 copy-done.4
  397.3 1.2 convolution_bitcast_fusion.6
  398.6 0.5 copy-done.3
  399.0 1.5 fusion.4
  400.6 44.2 %all-gather.8.cloned.1.call-done = bf16[8192,256]{1,0:T(8,128)(2,1)} async-done(((bf16[2048,256]{1,0:T(8,128)(2,1)}), bf16[8192,256]{1,0:T(8,128)(2,1)}) %all-gather.8.cloned.1.call-update) | async-done | bytes 4194320 | tf_op jit(solution)/shard_map/all_gather | solution.py:34
  444.8 16.9 %convolution_bitcast_fusion.1 = f32[2048,256]{0,1:T(8,128)} fusion(bf16[8192,256]{1,0:T(8,128)(2,1)} %all-gather.8.cloned.1.call-done, bf16[2048,8192]{1,0:T(8,128)(2,1)} %all-gather.6.cloned.1.call-done), kind=kOutput, calls=%fused_computation.3 | convolution fusion | flops 8589934592 | bytes 39845888 | tf_op jit(solution)/shard_map/dot_general | solution.py:32
  461.7 2.7 fusion.2
  464.5 1.0 copy-done.2
  465.4 1.2 convolution_bitcast_fusion.5
  466.6 2.3 copy.19
  468.9 2.5 copy.18
  471.4 48.7 %all-reduce.3.cloned.1.call-done = (f32[2,256,256]{2,1,0:T(8,128)}, f32[1,256,256]{2,1,0:T(8,128)}, f32[1,256,256]{2,1,0:T(8,128)}) async-done(((f32[2,256,256]{2,1,0:T(8,128)}, f32[1,256,256]{2,1,0:T(8,128)}, f32[1,256,256]{2,1,0:T(8,128)}), (f32[2,256,256]{2,1,0:T(8,128)}, f32[1,256,256]{2,1,0:T(8,128)}, f32[1,256,256]{2,1,0:T(8,128)})) %all-reduce.3.cloned.1.call-update) | async-done | bytes 1048592 | tf_op jit(solution)/shard_map/psum | solution.py:48
  520.1 1.4 fusion.6
  521.5 0.4 fusion.16
  521.9 0.2 fusion.12
  522.1 0.2 convolution_bitcast_fusion.2
  522.4 0.9 fusion.11
  (33 shorter events, 0.3 us)
Async XLA Ops:
  7.2 1.0 copy-start
  7.2 153.0 %all-gather.4.cloned.1.call-start = ((), (), s32[]{:S(2)}) async-start(), calls=%async_computation | async-start | bytes 10485760 | tf_op jit(solution)/shard_map/all_gather | solution.py:34
  12.0 1.7 copy-start.5
  12.1 1.7 copy-start.7
  12.1 352.2 %all-gather.6.cloned.1.call-start = ((), (), s32[]{:S(2)}) async-start(), calls=%async_computation.1 | async-start | bytes 41943040 | tf_op jit(solution)/shard_map/all_gather | solution.py:29
  12.8 2.5 copy-start.13
  12.8 3.7 copy-start.12
  12.8 432.0 %all-gather.8.cloned.1.call-start = ((), (), s32[]{:S(2)}) async-start(), calls=%async_computation.2 | async-start | bytes 5242880 | tf_op jit(solution)/shard_map/all_gather | solution.py:34
  15.2 504.9 %all-reduce.3.cloned.1.call-start = ((), (), s32[]{:S(2)}) async-start(), calls=%async_computation.3 | async-start | bytes 2097152 | tf_op jit(solution)/shard_map/psum | solution.py:48
  392.0 5.3 %copy-start.1 = (bf16[2048,256]{1,0:T(8,128)(2,1)S(1)}, bf16[2048,256]{1,0:T(8,128)(2,1)}, u32[]{:S(2)}) copy-start(bf16[2048,256]{1,0:T(8,128)(2,1)} %convolution_convert_fusion.1) | copy-start | bytes 3145732
  396.0 1.3 copy-start.4
  397.3 1.7 copy-start.3
  464.5 1.0 copy-start.2
  471.4 51.0 %copy-start.6 = (bf16[1,256,256]{2,1,0:T(8,128)(2,1)S(1)}, bf16[1,256,256]{2,1,0:T(8,128)(2,1)}, u32[]{:S(2)}) copy-start(bf16[1,256,256]{2,1,0:T(8,128)(2,1)} %param.16) | copy-start | bytes 393220
  520.1 1.8 copy-start.11
  520.1 2.3 copy-start.9
  521.5 1.8 copy-start.10
  522.1 1.2 copy-start.8
Sparse Core Ops, SparseCore 0:
  12.2 148.0 all-gather.3
  161.8 202.4 all-gather.5
  366.4 78.3 all-gather.7
  466.8 53.2 all-reduce.2
where the time goes:
time: 532 us; the launch traced here: 530 us
  waiting for transfers between devices  441 us (83%)
  matrix products  60.1 us (11%)
  between operations  14.6 us (3%)
  local copies, waits for them, and re-layouts  12.1 us (2%)
    all_gather x1, waiting for transfers between devices, per_device(): root_rows = lax.all_gather(sigma_root, 'col', axis=1, tiled=True)  204 us
    all_gather x2, waiting for transfers between devices, root_product(): lax.all_gather(panel, 'row', axis=0, tiled=True)  188 us
    psum x1, waiting for transfers between devices, per_device(): term1 = lax.psum(term1, 'row')  48.7 us
    dot_general x2, matrix products, root_product(): jnp.dot(root_rows, lax.all_gather(panel, 'row', axis=0, tiled=True), pref...  40.8 us
  transfers between devices with their start and end apart: 4, of which 4 were waited for; matrix products, arithmetic and copies ran while one was open for 8% of the time, Pallas kernels for 0%

commit v1 on v0

--- a/solution.py
+++ b/solution.py
@@ -81,7 +81,145 @@
     return (off1, diag1, off2, par2, diag2)
 
 
+def across(value, pairs):
+    return lax.ppermute(value, ("row", "col"), pairs)
+
+
+def place(side, step, core):
+    row = step if side == 0 else 3 - step
+    return 4 * row + 2 * side + core
+
+
+def hops(edges):
+    return [
+        (place(side, a, core), place(side, b, core))
+        for side in range(2)
+        for core in range(2)
+        for a, b in edges
+    ]
+
+
+def over(steps):
+    return [
+        (place(side, a, core), place(1 - side, 3 - a, core))
+        for side in range(2)
+        for core in range(2)
+        for a in steps
+    ]
+
+
+def swap_cores():
+    return [
+        (place(side, a, core), place(side, a, 1 - core))
+        for side in range(2)
+        for core in range(2)
+        for a in range(4)
+    ]
+
+
+def sum_rows(value):
+    for flip in (1, 3):
+        value = value + across(
+            value, [(4 * r + c, 4 * (r ^ flip) + c) for r in range(4) for c in range(4)]
+        )
+    return value
+
+
+def mul(a, b):
+    return jnp.dot(a, b, preferred_element_type=jnp.float32)
+
+
+def mul_t(a, b):
+    return lax.dot_general(a, b, (((0,), (0,)), ((), ())), preferred_element_type=jnp.float32)
+
+
+def per_device_chain(sigma_root, lower1, mask1, inv1, lower2, mask2, link2, inv2, parent):
+    bf16 = jnp.bfloat16
+    block = inv1.shape[1]
+    rows = sigma_root.shape[0]
+    row_blocks = rows // block
+    count1 = inv1.shape[0]
+    count2 = inv2.shape[0]
+    row_id = lax.axis_index("row")
+    col_id = lax.axis_index("col")
+    side, core = col_id // 2, col_id % 2
+    step = jnp.where(side == 0, row_id, 3 - row_id)
+    first = core == side
+
+    other = across(sigma_root, swap_cores())
+
+    def panels(lower, mask, inverse):
+        count = inverse.shape[0]
+        window = lax.dynamic_slice(mask, (row_id * row_blocks, col_id * count), (row_blocks, count))
+        out = []
+        for p in range(count):
+            piece = lower[:, p * block : (p + 1) * block].reshape(row_blocks, block, block)
+            masked = (piece * window[:, p].astype(bf16)[:, None, None]).reshape(rows, block)
+            out.append(mul(masked, inverse[p]).astype(bf16))
+        return out
+
+    def pick(a, b):
+        return jnp.where(first, a, b)
+
+    def root_product(v):
+        r1 = across(v, hops([(0, 1), (1, 2)]))
+        w = across(v, over([2, 3]))
+        q_own = mul_t(sigma_root, v)
+        d_own = across(q_own.astype(bf16), hops([(3, 2)]))
+        q_other = mul_t(other, v)
+        d_other = across(q_other.astype(bf16), hops([(3, 2)]))
+        r2 = across(r1, hops([(1, 2), (2, 3)]))
+        w_far = across(w, hops([(0, 1), (1, 0)]))
+        s_own = across((q_own + d_own).astype(bf16), hops([(2, 1)]))
+        s_other = across((q_other + d_other).astype(bf16), hops([(2, 1)]))
+        r3 = across(r2, hops([(2, 3)]))
+        w0 = jnp.where(step == 0, w, w_far)
+        w1 = jnp.where(step == 0, w_far, w)
+        g = mul(sigma_root, pick(w0, w1)) + mul(other, pick(w1, w0))
+        g = across(g.astype(bf16), over([0, 1]))
+        f0 = pick(s_own, s_other) + pick(q_own, q_other)
+        f0 = across(f0.astype(bf16), hops([(1, 0)]))
+        a = jnp.where(step == 0, v, jnp.where(step == 1, r1, jnp.where(step == 2, r2, r3)))
+        b = jnp.where(step == 1, v, jnp.where(step == 2, r1, jnp.where(step == 3, r2, 0)))
+        x = mul(sigma_root, pick(a, b)) + mul(other, pick(b, a))
+        rest = jnp.where(step == 0, f0, jnp.where(step == 1, pick(s_other, s_own), g))
+        return x + rest
+
+    u1 = panels(lower1, mask1, inv1)
+    u2 = panels(lower2, mask2, inv2)
+    off1 = [(-root_product(u)).astype(bf16) for u in u1]
+    term1 = sum_rows(jnp.stack([mul_t(u, o) for u, o in zip(u1, off1)]))
+    base1 = jnp.stack([mul_t(inv1[p], inv1[p]) for p in range(count1)])
+    diag1 = (base1 - term1).astype(bf16)
+    off2, par2, diag2 = [], [], []
+    for k in range(count2):
+        which = lax.dynamic_index_in_dim(parent, col_id * count2 + k, keepdims=False)
+        which = which - col_id * count1
+        par_off, par_diag = off1[0], diag1[0]
+        for p in range(1, count1):
+            par_off = jnp.where(which == p, off1[p], par_off)
+            par_diag = jnp.where(which == p, diag1[p], par_diag)
+        link_u = mul(link2[k], inv2[k]).astype(bf16)
+        cross = sum_rows(mul_t(par_off, u2[k]))
+        par = (-(cross + mul(par_diag, link_u))).astype(bf16)
+        known = mul_t(inv2[k], inv2[k]) - mul_t(link_u, par)
+        o2 = (-(root_product(u2[k]) + mul(par_off, link_u))).astype(bf16)
+        pair = sum_rows(mul_t(u2[k], o2))
+        off2.append(o2)
+        par2.append(par)
+        diag2.append((known - pair).astype(bf16))
+    return (
+        jnp.concatenate(off1, axis=1),
+        diag1,
+        jnp.concatenate(off2, axis=1),
+        jnp.stack(par2),
+        jnp.stack(diag2),
+    )
+
+
 def solution(mesh):
+    chain = mesh.shape["row"] == 4 and mesh.shape["col"] == 4
+    body = per_device_chain if chain else per_device
     placed = (
         P(("hyp", "row"), "col"),
         P(("hyp", "row"), "col"),
@@ -94,7 +232,7 @@
         P(),
     )
     return jax.shard_map(
-        per_device,
+        body,
         mesh=mesh,
         in_specs=placed,
         out_specs=(

time: 532 us -> 475 us (0.89); the launches traced: 530 us -> 467 us
  waiting for transfers between devices: 441 us -> 200 us
  starting transfers between devices: 0.16 us -> 110 us
  matrix products: 60.1 us -> 135 us
  other arithmetic: 1.56 us -> 17.5 us
  between operations: 14.6 us -> 2.55 us
  local copies, waits for them, and re-layouts: 12.1 us -> 1.75 us
    all_gather x3 -> x0, waiting for transfers between devices: 392 us -> none  [the longest x1 204 us: per_device(): root_rows = lax.all_gather(sigma_root, 'col', axis=1, tiled=True)]
    ppermute x0 -> x40, waiting for transfers between devices: none -> 200 us  [across(): return lax.ppermute(value, ('row', 'col'), pairs)]
    ppermute x0 -> x40, starting transfers between devices: none -> 110 us  [across(): return lax.ppermute(value, ('row', 'col'), pairs)]
    dot_general x15 -> x32, matrix products: 60.1 us -> 135 us  [the longest x18 83.2 us: mul(): return jnp.dot(a, b, preferred_element_type=jnp.float32)]
    psum x1 -> x0, waiting for transfers between devices: 48.7 us -> none  [per_device(): term1 = lax.psum(term1, 'row')]
    convert_element_type x1 -> x11, other arithmetic: 0.8 us -> 11.6 us  [the longest x3 5.45 us: root_product(): f0 = across(f0.astype(bf16), hops([(1, 0)]))]
    unnamed x34 -> x57, local copies, waits for them, and re-layouts: 7.71 us -> 1.16 us
  transfers between devices with their start and end apart: 4 -> 40, of which waited for: 4 -> 16; matrix products, arithmetic and copies ran while one was open for 8% -> 33% of each run, Pallas kernels for 0% -> 0%
where the time goes in v1:
time: 475 us; the launch traced here: 467 us
  waiting for transfers between devices  200 us (42%)
  matrix products  135 us (28%)
  starting transfers between devices  110 us (23%)
  other arithmetic  17.5 us (4%)
    ppermute x40, waiting for transfers between devices, across(): return lax.ppermute(value, ('row', 'col'), pairs)  200 us
    ppermute x40, starting transfers between devices, across(): return lax.ppermute(value, ('row', 'col'), pairs)  110 us
    dot_general x18, matrix products, mul(): return jnp.dot(a, b, preferred_element_type=jnp.float32)  83.2 us
    dot_general x14, matrix products, mul_t(): lax.dot_general(a, b, (((0,), (0,)), ((), ())), preferred_element_type=jn...  51.8 us
  transfers between devices with their start and end apart: 40, of which 16 were waited for; matrix products, arithmetic and copies ran while one was open for 33% of the time, Pallas kernels for 0%

profile of v1, /device:TPU:10, one launch (start us, length us, event | category | flops | bytes accessed | tf_op | source)
XLA Modules:
  0.0 466.6 jit_solution(15962765598963987335)
XLA Ops:
  7.3 8.5 %fusion.86 = (bf16[2048,256]{1,0:T(8,128)(2,1)}, f32[2048,256]{1,0:T(8,128)}) fusion(bf16[2048,256]{1,0:T(8,128)(2,1)S(1)} %convolution_convert_fusion.2, bf16[2048,2048]{1,0:T(8,128)(2,1)} %param.9), kind=kOutput, calls=%fused_computation.138 | convolution fusion | flops 2148007936 | bytes 12582912 | tf_op jit(solution)/shard_map/dot_general | solution.py:133
  21.0 5.6 %fusion.84 = (bf16[2048,256]{1,0:T(8,128)(2,1)}, f32[2048,256]{1,0:T(8,128)S(1)}) fusion(bf16[2048,256]{1,0:T(8,128)(2,1)} %convolution_convert_fusion.1, bf16[2048,2048]{1,0:T(8,128)(2,1)S(1)} %bitcast.136), kind=kOutput, calls=%fused_computation.136 | convolution fusion | flops 2148007936 | bytes 12582912 | tf_op jit(solution)/shard_map/dot_general | solution.py:133
  36.9 8.6 %collective-permute-start.25 = (bf16[2048,256]{1,0:T(8,128)(2,1)S(1)}, bf16[2048,256]{1,0:T(8,128)(2,1)S(1)}, u32[]{:S(2)}, u32[]{:S(2)}) collective-permute-start(bf16[2048,256]{1,0:T(8,128)(2,1)S(1)} %convolution_convert_fusion), channel_id=1, source_target_pairs={{0,4},{4,8},{1,5},{5,9},{14,10},{10,6},{15,11},{11,7},{16,20},{20,... | collective-permute-start | bytes 3145736 | tf_op jit(solution)/shard_map/ppermute | solution.py:85
  47.1 6.8 %fusion.88 = (bf16[2048,256]{1,0:T(8,128)(2,1)S(1)}, f32[2048,256]{1,0:T(8,128)S(1)}) fusion(bf16[2048,256]{1,0:T(8,128)(2,1)S(1)} %convolution_convert_fusion, bf16[2048,2048]{1,0:T(8,128)(2,1)} %param.9), kind=kOutput, calls=%fused_computation.140 | convolution fusion | flops 2148007936 | bytes 12582912 | tf_op jit(solution)/shard_map/dot_general | solution.py:133
  54.6 14.3 %collective-permute-start.13 = (bf16[2048,256]{1,0:T(8,128)(2,1)}, bf16[2048,256]{1,0:T(8,128)(2,1)S(1)}, u32[]{:S(2)}, u32[]{:S(2)}) collective-permute-start(bf16[2048,256]{1,0:T(8,128)(2,1)} %collective-permute-done.12), channel_id=1, source_target_pairs={{4,8},{8,12},{5,9},{9,13},{10,6},{6,2},{11,7},{7,3},{20,24},{24,28... | collective-permute-start | bytes 3145736 | tf_op jit(solution)/shard_map/ppermute | solution.py:85
  70.4 5.8 %collective-permute-done.25 = bf16[2048,256]{1,0:T(8,128)(2,1)S(1)} collective-permute-done((bf16[2048,256]{1,0:T(8,128)(2,1)S(1)}, bf16[2048,256]{1,0:T(8,128)(2,1)S(1)}, u32[]{:S(2)}, u32[]{:S(2)}) %collective-permute-start.25) | collective-permute-done | bytes 1048608 | tf_op jit(solution)/shard_map/ppermute | solution.py:85
  80.1 18.1 %collective-permute-done.1 = bf16[2048,256]{1,0:T(8,128)(2,1)S(1)} collective-permute-done((bf16[2048,256]{1,0:T(8,128)(2,1)}, bf16[2048,256]{1,0:T(8,128)(2,1)S(1)}, u32[]{:S(2)}, u32[]{:S(2)}) %collective-permute-start.1) | collective-permute-done | bytes 1048608 | tf_op jit(solution)/shard_map/ppermute | solution.py:85
  101.7 19.0 %collective-permute-done.13 = bf16[2048,256]{1,0:T(8,128)(2,1)S(1)} collective-permute-done((bf16[2048,256]{1,0:T(8,128)(2,1)}, bf16[2048,256]{1,0:T(8,128)(2,1)S(1)}, u32[]{:S(2)}, u32[]{:S(2)}) %collective-permute-start.13) | collective-permute-done | bytes 1048608 | tf_op jit(solution)/shard_map/ppermute | solution.py:85
  121.7 21.0 %collective-permute-done.26 = bf16[2048,256]{1,0:T(8,128)(2,1)S(1)} collective-permute-done((bf16[2048,256]{1,0:T(8,128)(2,1)S(1)}, bf16[2048,256]{1,0:T(8,128)(2,1)S(1)}, u32[]{:S(2)}, u32[]{:S(2)}) %collective-permute-start.26) | collective-permute-done | bytes 1048608 | tf_op jit(solution)/shard_map/ppermute | solution.py:85
  152.7 18.0 %collective-permute-done.20 = bf16[2048,256]{1,0:T(8,128)(2,1)S(1)} collective-permute-done((bf16[2048,256]{1,0:T(8,128)(2,1)}, bf16[2048,256]{1,0:T(8,128)(2,1)S(1)}, u32[]{:S(2)}, u32[]{:S(2)}) %collective-permute-start.20) | collective-permute-done | bytes 1048608 | tf_op jit(solution)/shard_map/ppermute | solution.py:85
  172.1 20.4 %collective-permute-done.33 = bf16[2048,256]{1,0:T(8,128)(2,1)} collective-permute-done((bf16[2048,256]{1,0:T(8,128)(2,1)S(1)}, bf16[2048,256]{1,0:T(8,128)(2,1)}, u32[]{:S(2)}, u32[]{:S(2)}) %collective-permute-start.33) | collective-permute-done | bytes 1048608 | tf_op jit(solution)/shard_map/ppermute | solution.py:85
  199.9 7.1 %fusion.37 = f32[256,2048]{0,1:T(8,128)} fusion(bf16[2048,2048]{1,0:T(8,128)(2,1)} %collective-permute-done.3, pred[]{:T(512)S(6)} %eq.16, bf16[2048,256]{1,0:T(8,128)(2,1)S(1)} %collective-permute-done.9, bf16[2048,256]{1,0:T(8,128)(2,1)S(1)} %collective-permute-done.10, pred[]{:T(512)S(6)} %eq.18), kind=kOutput, calls=%fused_computation.72 | convolution fusion | flops 2149056512 | bytes 12582914 | tf_op jit(solution)/shard_map/dot_general | solution.py:129
  206.9 6.8 %fusion.87 = (bf16[2048,256]{1,0:T(8,128)(2,1)S(1)}, f32[2048,256]{1,0:T(8,128)S(1)}) fusion(bf16[2048,256]{1,0:T(8,128)(2,1)S(1)} %convolution_convert_fusion.2, bf16[2048,2048]{1,0:T(8,128)(2,1)} %collective-permute-done.3), kind=kOutput, calls=%fused_computation.139 | convolution fusion | flops 2148007936 | bytes 12582912 | tf_op jit(solution)/shard_map/dot_general | solution.py:133
  213.8 7.3 %fusion.18 = bf16[2048,256]{1,0:T(8,128)(2,1)} fusion(f32[256,2048]{0,1:T(8,128)} %fusion.37, bf16[2048,2048]{1,0:T(8,128)(2,1)} %param.9, pred[]{:T(512)S(6)} %eq.16, bf16[2048,256]{1,0:T(8,128)(2,1)S(1)} %collective-permute-done.9, bf16[2048,256]{1,0:T(8,128)(2,1)S(1)} %copy-done.15, pred[]{:T(512)S(6)} %eq.18), kind=kOutput, calls=%fused_computation.33 | convolution fusion | flops 2150105088 | bytes 13631490 | tf_op jit(solution)/shard_map/dot_general | solution.py:129
  222.9 7.1 %fusion.29 = f32[256,2048]{0,1:T(8,128)} fusion(bf16[2048,2048]{1,0:T(8,128)(2,1)} %collective-permute-done.3, pred[]{:T(512)S(6)} %eq.16, bf16[2048,256]{1,0:T(8,128)(2,1)S(1)} %collective-permute-done.20, bf16[2048,256]{1,0:T(8,128)(2,1)S(1)} %collective-permute-done.21, pred[]{:T(512)S(6)} %eq.18), kind=kOutput, calls=%fused_computation.62 | convolution fusion | flops 2149056512 | bytes 12582914 | tf_op jit(solution)/shard_map/dot_general | solution.py:129
  230.0 8.2 %fusion.85 = (bf16[2048,256]{1,0:T(8,128)(2,1)}, f32[2048,256]{1,0:T(8,128)S(1)}) fusion(bf16[2048,256]{1,0:T(8,128)(2,1)} %convolution_convert_fusion.1, bf16[2048,2048]{1,0:T(8,128)(2,1)} %collective-permute-done.3), kind=kOutput, calls=%fused_computation.137 | convolution fusion | flops 2148007936 | bytes 12582912 | tf_op jit(solution)/shard_map/dot_general | solution.py:133
  238.2 7.3 %fusion.17 = bf16[2048,256]{1,0:T(8,128)(2,1)} fusion(f32[256,2048]{0,1:T(8,128)} %fusion.29, bf16[2048,2048]{1,0:T(8,128)(2,1)} %param.9, pred[]{:T(512)S(6)} %eq.16, bf16[2048,256]{1,0:T(8,128)(2,1)S(1)} %collective-permute-done.20, bf16[2048,256]{1,0:T(8,128)(2,1)S(1)} %copy-done.17, pred[]{:T(512)S(6)} %eq.18), kind=kOutput, calls=%fused_computation.32 | convolution fusion | flops 2150105088 | bytes 13631490 | tf_op jit(solution)/shard_map/dot_general | solution.py:129
  247.4 7.0 %fusion.22 = f32[256,2048]{0,1:T(8,128)S(1)} fusion(bf16[2048,2048]{1,0:T(8,128)(2,1)} %collective-permute-done.3, pred[]{:T(512)S(6)} %eq.16, bf16[2048,256]{1,0:T(8,128)(2,1)} %collective-permute-done.33, bf16[2048,256]{1,0:T(8,128)(2,1)} %collective-permute-done.34, pred[]{:T(512)S(6)} %eq.18), kind=kOutput, calls=%fused_computation.53 | convolution fusion | flops 2149056512 | bytes 12582914 | tf_op jit(solution)/shard_map/dot_general | solution.py:129
  259.4 7.2 %fusion.40 = f32[256,2048]{0,1:T(8,128)} fusion(bf16[2048,2048]{1,0:T(8,128)(2,1)} %collective-permute-done.3, bf16[2048,256]{1,0:T(8,128)(2,1)S(1)} %get-tuple-element.8, bf16[2048,256]{1,0:T(8,128)(2,1)S(1)} %get-tuple-element.7, pred[]{:T(512)S(6)} %eq.16), kind=kOutput, calls=%fused_computation.75 | convolution fusion | flops 2148007936 | bytes 12582913 | tf_op jit(solution)/shard_map/dot_general | solution.py:129
  266.6 7.1 %fusion.32 = f32[256,2048]{0,1:T(8,128)} fusion(bf16[2048,2048]{1,0:T(8,128)(2,1)} %collective-permute-done.3, bf16[2048,256]{1,0:T(8,128)(2,1)S(1)} %get-tuple-element.10, bf16[2048,256]{1,0:T(8,128)(2,1)S(1)} %get-tuple-element.9, pred[]{:T(512)S(6)} %eq.16), kind=kOutput, calls=%fused_computation.65 | convolution fusion | flops 2148007936 | bytes 12582913 | tf_op jit(solution)/shard_map/dot_general | solution.py:129
  273.6 7.1 %fusion.25 = f32[256,2048]{0,1:T(8,128)} fusion(bf16[2048,2048]{1,0:T(8,128)(2,1)} %collective-permute-done.3, bf16[2048,256]{1,0:T(8,128)(2,1)S(1)} %get-tuple-element.6, bf16[2048,256]{1,0:T(8,128)(2,1)S(1)} %get-tuple-element.5, pred[]{:T(512)S(6)} %eq.16), kind=kOutput, calls=%fused_computation.56 | convolution fusion | flops 2148007936 | bytes 12582913 | tf_op jit(solution)/shard_map/dot_general | solution.py:129
  280.7 8.0 %fusion.89 = (bf16[2048,256]{1,0:T(8,128)(2,1)}, f32[2048,256]{1,0:T(8,128)S(1)}) fusion(bf16[2048,256]{1,0:T(8,128)(2,1)S(1)} %convolution_convert_fusion, bf16[2048,2048]{1,0:T(8,128)(2,1)} %collective-permute-done.3), kind=kOutput, calls=%fused_computation.141 | convolution fusion | flops 2148007936 | bytes 12582912 | tf_op jit(solution)/shard_map/dot_general | solution.py:133
  295.0 24.3 %collective-permute-start.11 = (bf16[2048,256]{1,0:T(8,128)(2,1)S(1)}, bf16[2048,256]{1,0:T(8,128)(2,1)S(1)}, u32[]{:S(2)}, u32[]{:S(2)}) collective-permute-start(bf16[2048,256]{1,0:T(8,128)(2,1)S(1)} %copy-done.12), channel_id=1, source_target_pairs={{0,2},{4,6},{1,3},{5,7},{14,12},{10,8},{15,13},{11,9},{16,18},{20,... | collective-permute-start | bytes 3145736 | tf_op jit(solution)/shard_map/ppermute | solution.py:85
  327.1 13.3 %collective-permute-done.18 = bf16[2048,256]{1,0:T(8,128)(2,1)S(1)} collective-permute-done((bf16[2048,256]{1,0:T(8,128)(2,1)S(1)}, bf16[2048,256]{1,0:T(8,128)(2,1)S(1)}, u32[]{:S(2)}, u32[]{:S(2)}) %collective-permute-start.18) | collective-permute-done | bytes 1048608 | tf_op jit(solution)/shard_map/ppermute | solution.py:85
  344.9 15.2 %collective-permute-done.31 = bf16[2048,256]{1,0:T(8,128)(2,1)S(1)} collective-permute-done((bf16[2048,256]{1,0:T(8,128)(2,1)S(1)}, bf16[2048,256]{1,0:T(8,128)(2,1)S(1)}, u32[]{:S(2)}, u32[]{:S(2)}) %collective-permute-start.31) | collective-permute-done | bytes 1048608 | tf_op jit(solution)/shard_map/ppermute | solution.py:85
  365.0 6.9 %fusion.14 = bf16[2048,256]{1,0:T(8,128)(2,1)S(1)} fusion(f32[256,2048]{0,1:T(8,128)} %fusion.40, bf16[2048,2048]{1,0:T(8,128)(2,1)} %param.9, bf16[2048,256]{1,0:T(8,128)(2,1)S(1)} %collective-permute-done.8, bf16[2048,256]{1,0:T(8,128)(2,1)} %copy-done.13, bf16[2048,256]{1,0:T(8,128)(2,1)S(1)} %collective-permute-done.7, ...), kind=kOutput, calls=%fused_computation.29 | convolution fusion | flops 2152202240 | bytes 17825796 | tf_op jit(solution)/shard_map/dot_general | solution.py:129
  371.9 13.1 %collective-permute-done.19 = bf16[2048,256]{1,0:T(8,128)(2,1)S(1)} collective-permute-done((bf16[2048,256]{1,0:T(8,128)(2,1)S(1)}, bf16[2048,256]{1,0:T(8,128)(2,1)S(1)}, u32[]{:S(2)}, u32[]{:S(2)}) %collective-permute-start.19) | collective-permute-done | bytes 1048608 | tf_op jit(solution)/shard_map/ppermute | solution.py:85
  395.7 11.8 %collective-permute-done.32 = bf16[2048,256]{1,0:T(8,128)(2,1)S(1)} collective-permute-done((bf16[2048,256]{1,0:T(8,128)(2,1)S(1)}, bf16[2048,256]{1,0:T(8,128)(2,1)S(1)}, u32[]{:S(2)}, u32[]{:S(2)}) %collective-permute-start.32) | collective-permute-done | bytes 1048608 | tf_op jit(solution)/shard_map/ppermute | solution.py:85
  410.5 10.4 %collective-permute-done.23 = f32[2,256,256]{2,1,0:T(8,128)S(1)} collective-permute-done((f32[2,256,256]{2,1,0:T(8,128)S(1)}, f32[2,256,256]{2,1,0:T(8,128)S(1)}, u32[]{:S(2)}, u32[]{:S(2)}) %collective-permute-start.23) | collective-permute-done | bytes 524320 | tf_op jit(solution)/shard_map/ppermute | solution.py:85
  428.6 12.2 %collective-permute-done.38 = f32[256,256]{1,0:T(8,128)S(1)} collective-permute-done((f32[256,256]{1,0:T(8,128)S(1)}, f32[256,256]{1,0:T(8,128)S(1)}, u32[]{:S(2)}, u32[]{:S(2)}) %collective-permute-start.38) | collective-permute-done | bytes 262176 | tf_op jit(solution)/shard_map/ppermute | solution.py:85
  443.6 13.5 %collective-permute-done.24 = f32[2,256,256]{2,1,0:T(8,128)S(1)} collective-permute-done((f32[2,256,256]{2,1,0:T(8,128)S(1)}, f32[2,256,256]{2,1,0:T(8,128)S(1)}, u32[]{:S(2)}, u32[]{:S(2)}) %collective-permute-start.24) | collective-permute-done | bytes 524320 | tf_op jit(solution)/shard_map/ppermute | solution.py:85
  457.3 5.2 %collective-permute-done.37 = f32[256,256]{1,0:T(8,128)S(1)} collective-permute-done((f32[256,256]{1,0:T(8,128)S(1)}, f32[256,256]{1,0:T(8,128)S(1)}, u32[]{:S(2)}, u32[]{:S(2)}) %collective-permute-start.37) | collective-permute-done | bytes 262176 | tf_op jit(solution)/shard_map/ppermute | solution.py:85
  (162 shorter events, 112.1 us)
Async XLA Ops:
  0.6 195.0 %collective-permute-start.3 = (bf16[2048,2048]{1,0:T(8,128)(2,1)}, bf16[2048,2048]{1,0:T(8,128)(2,1)}, u32[]{:S(2)}, u32[]{:S(2)}) collective-permute-start(bf16[2048,2048]{1,0:T(8,128)(2,1)} %param.9), channel_id=1, source_target_pairs={{0,1},{4,5},{8,9},{12,13},{1,0},{5,4},{9,8},{13,12},{14,15},{10,11... | collective-permute-start | bytes 25165832 | tf_op jit(solution)/shard_map/ppermute | solution.py:85
  3.5 42.0 %collective-permute-start = (bf16[2048,256]{1,0:T(8,128)(2,1)S(1)}, bf16[2048,256]{1,0:T(8,128)(2,1)}, u32[]{:S(2)}, u32[]{:S(2)}) collective-permute-start(bf16[2048,256]{1,0:T(8,128)(2,1)S(1)} %convolution_convert_fusion.2), channel_id=1, source_target_pairs={{0,4},{4,8},{1,5},{5,9},{14,10},{10,6},{15,11},{11,7},{16,20},{20,... | collective-permute-start | bytes 3145736 | tf_op jit(solution)/shard_map/ppermute | solution.py:85
  18.9 35.7 %collective-permute-start.12 = (bf16[2048,256]{1,0:T(8,128)(2,1)}, bf16[2048,256]{1,0:T(8,128)(2,1)}, u32[]{:S(2)}, u32[]{:S(2)}) collective-permute-start(bf16[2048,256]{1,0:T(8,128)(2,1)} %convolution_convert_fusion.1), channel_id=1, source_target_pairs={{0,4},{4,8},{1,5},{5,9},{14,10},{10,6},{15,11},{11,7},{16,20},{20,... | collective-permute-start | bytes 3145736 | tf_op jit(solution)/shard_map/ppermute | solution.py:85
  26.6 27.3 %collective-permute-start.15 = (bf16[2048,256]{1,0:T(8,128)(2,1)}, bf16[2048,256]{1,0:T(8,128)(2,1)}, u32[]{:S(2)}, u32[]{:S(2)}) collective-permute-start(bf16[2048,256]{1,0:T(8,128)(2,1)} %get-tuple-element.13), channel_id=1, source_target_pairs={{12,8},{13,9},{2,6},{3,7},{28,24},{29,25},{18,22},{19,23}} | collective-permute-start | bytes 3145736 | tf_op jit(solution)/shard_map/ppermute | solution.py:85
  36.9 39.3 %collective-permute-start.25 = (bf16[2048,256]{1,0:T(8,128)(2,1)S(1)}, bf16[2048,256]{1,0:T(8,128)(2,1)S(1)}, u32[]{:S(2)}, u32[]{:S(2)}) collective-permute-start(bf16[2048,256]{1,0:T(8,128)(2,1)S(1)} %convolution_convert_fusion), channel_id=1, source_target_pairs={{0,4},{4,8},{1,5},{5,9},{14,10},{10,6},{15,11},{11,7},{16,20},{20,... | collective-permute-start | bytes 3145736 | tf_op jit(solution)/shard_map/ppermute | solution.py:85
  45.5 52.7 %collective-permute-start.1 = (bf16[2048,256]{1,0:T(8,128)(2,1)}, bf16[2048,256]{1,0:T(8,128)(2,1)S(1)}, u32[]{:S(2)}, u32[]{:S(2)}) collective-permute-start(bf16[2048,256]{1,0:T(8,128)(2,1)} %collective-permute-done), channel_id=1, source_target_pairs={{4,8},{8,12},{5,9},{9,13},{10,6},{6,2},{11,7},{7,3},{20,24},{24,28... | collective-permute-start | bytes 3145736 | tf_op jit(solution)/shard_map/ppermute | solution.py:85
  53.8 46.6 %collective-permute-start.28 = (bf16[2048,256]{1,0:T(8,128)(2,1)S(1)}, bf16[2048,256]{1,0:T(8,128)(2,1)S(1)}, u32[]{:S(2)}, u32[]{:S(2)}) collective-permute-start(bf16[2048,256]{1,0:T(8,128)(2,1)S(1)} %get-tuple-element.21), channel_id=1, source_target_pairs={{12,8},{13,9},{2,6},{3,7},{28,24},{29,25},{18,22},{19,23}} | collective-permute-start | bytes 3145736 | tf_op jit(solution)/shard_map/ppermute | solution.py:85
  54.6 66.1 %collective-permute-start.13 = (bf16[2048,256]{1,0:T(8,128)(2,1)}, bf16[2048,256]{1,0:T(8,128)(2,1)S(1)}, u32[]{:S(2)}, u32[]{:S(2)}) collective-permute-start(bf16[2048,256]{1,0:T(8,128)(2,1)} %collective-permute-done.12), channel_id=1, source_target_pairs={{4,8},{8,12},{5,9},{9,13},{10,6},{6,2},{11,7},{7,3},{20,24},{24,28... | collective-permute-start | bytes 3145736 | tf_op jit(solution)/shard_map/ppermute | solution.py:85
  76.2 66.5 %collective-permute-start.26 = (bf16[2048,256]{1,0:T(8,128)(2,1)S(1)}, bf16[2048,256]{1,0:T(8,128)(2,1)S(1)}, u32[]{:S(2)}, u32[]{:S(2)}) collective-permute-start(bf16[2048,256]{1,0:T(8,128)(2,1)S(1)} %collective-permute-done.25), channel_id=1, source_target_pairs={{4,8},{8,12},{5,9},{9,13},{10,6},{6,2},{11,7},{7,3},{20,24},{24,28... | collective-permute-start | bytes 3145736 | tf_op jit(solution)/shard_map/ppermute | solution.py:85
  98.2 45.7 %collective-permute-start.2 = (bf16[2048,256]{1,0:T(8,128)(2,1)S(1)}, bf16[2048,256]{1,0:T(8,128)(2,1)S(1)}, u32[]{:S(2)}, u32[]{:S(2)}) collective-permute-start(bf16[2048,256]{1,0:T(8,128)(2,1)S(1)} %collective-permute-done.1), channel_id=1, source_target_pairs={{8,12},{9,13},{6,2},{7,3},{24,28},{25,29},{22,18},{23,19}} | collective-permute-start | bytes 3145736 | tf_op jit(solution)/shard_map/ppermute | solution.py:85
  100.4 45.7 %collective-permute-start.9 = (bf16[2048,256]{1,0:T(8,128)(2,1)S(1)}, bf16[2048,256]{1,0:T(8,128)(2,1)S(1)}, u32[]{:S(2)}, u32[]{:S(2)}) collective-permute-start(bf16[2048,256]{1,0:T(8,128)(2,1)S(1)} %convolution_convert_fusion.2), channel_id=1, source_target_pairs={{8,10},{12,14},{9,11},{13,15},{6,4},{2,0},{7,5},{3,1},{24,26},{28,... | collective-permute-start | bytes 3145736 | tf_op jit(solution)/shard_map/ppermute | solution.py:85
  120.7 26.8 %collective-permute-start.14 = (bf16[2048,256]{1,0:T(8,128)(2,1)S(1)}, bf16[2048,256]{1,0:T(8,128)(2,1)S(1)}, u32[]{:S(2)}, u32[]{:S(2)}) collective-permute-start(bf16[2048,256]{1,0:T(8,128)(2,1)S(1)} %collective-permute-done.13), channel_id=1, source_target_pairs={{8,12},{9,13},{6,2},{7,3},{24,28},{25,29},{22,18},{23,19}} | collective-permute-start | bytes 3145736 | tf_op jit(solution)/shard_map/ppermute | solution.py:85
  142.7 28.1 %collective-permute-start.20 = (bf16[2048,256]{1,0:T(8,128)(2,1)}, bf16[2048,256]{1,0:T(8,128)(2,1)S(1)}, u32[]{:S(2)}, u32[]{:S(2)}) collective-permute-start(bf16[2048,256]{1,0:T(8,128)(2,1)} %convolution_convert_fusion.1), channel_id=1, source_target_pairs={{8,10},{12,14},{9,11},{13,15},{6,4},{2,0},{7,5},{3,1},{24,26},{28,... | collective-permute-start | bytes 3145736 | tf_op jit(solution)/shard_map/ppermute | solution.py:85
  146.2 46.3 %collective-permute-start.33 = (bf16[2048,256]{1,0:T(8,128)(2,1)S(1)}, bf16[2048,256]{1,0:T(8,128)(2,1)}, u32[]{:S(2)}, u32[]{:S(2)}) collective-permute-start(bf16[2048,256]{1,0:T(8,128)(2,1)S(1)} %convolution_convert_fusion), channel_id=1, source_target_pairs={{8,10},{12,14},{9,11},{13,15},{6,4},{2,0},{7,5},{3,1},{24,26},{28,... | collective-permute-start | bytes 3145736 | tf_op jit(solution)/shard_map/ppermute | solution.py:85
  147.5 46.3 %collective-permute-start.10 = (bf16[2048,256]{1,0:T(8,128)(2,1)S(1)}, bf16[2048,256]{1,0:T(8,128)(2,1)S(1)}, u32[]{:S(2)}, u32[]{:S(2)}) collective-permute-start(bf16[2048,256]{1,0:T(8,128)(2,1)S(1)} %collective-permute-done.9), channel_id=1, source_target_pairs={{0,4},{4,0},{1,5},{5,1},{14,10},{10,14},{15,11},{11,15},{16,20},{2... | collective-permute-start | bytes 3145736 | tf_op jit(solution)/shard_map/ppermute | solution.py:85
  151.2 142.9 %collective-permute-start.5 = (bf16[2048,256]{1,0:T(8,128)(2,1)S(1)}, bf16[2048,256]{1,0:T(8,128)(2,1)}, u32[]{:S(2)}, u32[]{:S(2)}) collective-permute-start(bf16[2048,256]{1,0:T(8,128)(2,1)S(1)} %add_convert_fusion.8), channel_id=1, source_target_pairs={{8,4},{9,5},{6,10},{7,11},{24,20},{25,21},{22,26},{23,27}} | collective-permute-start | bytes 3145736 | tf_op jit(solution)/shard_map/ppermute | solution.py:85
  170.8 151.6 %collective-permute-start.16 = (bf16[2048,256]{1,0:T(8,128)(2,1)S(1)}, bf16[2048,256]{1,0:T(8,128)(2,1)}, u32[]{:S(2)}, u32[]{:S(2)}) collective-permute-start(bf16[2048,256]{1,0:T(8,128)(2,1)S(1)} %add_convert_fusion.5), channel_id=1, source_target_pairs={{8,4},{9,5},{6,10},{7,11},{24,20},{25,21},{22,26},{23,27}} | collective-permute-start | bytes 3145736 | tf_op jit(solution)/shard_map/ppermute | solution.py:85
  192.4 151.1 %collective-permute-start.29 = (bf16[2048,256]{1,0:T(8,128)(2,1)S(1)}, bf16[2048,256]{1,0:T(8,128)(2,1)}, u32[]{:S(2)}, u32[]{:S(2)}) collective-permute-start(bf16[2048,256]{1,0:T(8,128)(2,1)S(1)} %add_convert_fusion.2), channel_id=1, source_target_pairs={{8,4},{9,5},{6,10},{7,11},{24,20},{25,21},{22,26},{23,27}} | collective-permute-start | bytes 3145736 | tf_op jit(solution)/shard_map/ppermute | solution.py:85
  193.7 28.0 %collective-permute-start.21 = (bf16[2048,256]{1,0:T(8,128)(2,1)S(1)}, bf16[2048,256]{1,0:T(8,128)(2,1)S(1)}, u32[]{:S(2)}, u32[]{:S(2)}) collective-permute-start(bf16[2048,256]{1,0:T(8,128)(2,1)S(1)} %collective-permute-done.20), channel_id=1, source_target_pairs={{0,4},{4,0},{1,5},{5,1},{14,10},{10,14},{15,11},{11,15},{16,20},{2... | collective-permute-start | bytes 3145736 | tf_op jit(solution)/shard_map/ppermute | solution.py:85
  195.7 49.8 %collective-permute-start.34 = (bf16[2048,256]{1,0:T(8,128)(2,1)}, bf16[2048,256]{1,0:T(8,128)(2,1)}, u32[]{:S(2)}, u32[]{:S(2)}) collective-permute-start(bf16[2048,256]{1,0:T(8,128)(2,1)} %collective-permute-done.33), channel_id=1, source_target_pairs={{0,4},{4,0},{1,5},{5,1},{14,10},{10,14},{15,11},{11,15},{16,20},{2... | collective-permute-start | bytes 3145736 | tf_op jit(solution)/shard_map/ppermute | solution.py:85
  221.7 67.0 %collective-permute-start.6 = (bf16[2048,256]{1,0:T(8,128)(2,1)S(1)}, bf16[2048,256]{1,0:T(8,128)(2,1)S(1)}, u32[]{:S(2)}, u32[]{:S(2)}) collective-permute-start(bf16[2048,256]{1,0:T(8,128)(2,1)S(1)} %get-tuple-element.19), channel_id=1, source_target_pairs={{12,8},{13,9},{2,6},{3,7},{28,24},{29,25},{18,22},{19,23}} | collective-permute-start | bytes 3145736 | tf_op jit(solution)/shard_map/ppermute | solution.py:85
  245.5 44.2 %collective-permute-start.17 = (bf16[2048,256]{1,0:T(8,128)(2,1)}, bf16[2048,256]{1,0:T(8,128)(2,1)}, u32[]{:S(2)}, u32[]{:S(2)}) collective-permute-start(bf16[2048,256]{1,0:T(8,128)(2,1)} %get-tuple-element.15), channel_id=1, source_target_pairs={{12,8},{13,9},{2,6},{3,7},{28,24},{29,25},{18,22},{19,23}} | collective-permute-start | bytes 3145736 | tf_op jit(solution)/shard_map/ppermute | solution.py:85
  289.7 29.6 %collective-permute-start.7 = (bf16[2048,256]{1,0:T(8,128)(2,1)S(1)}, bf16[2048,256]{1,0:T(8,128)(2,1)S(1)}, u32[]{:S(2)}, u32[]{:S(2)}) collective-permute-start(bf16[2048,256]{1,0:T(8,128)(2,1)S(1)} %add_convert_fusion.7), channel_id=1, source_target_pairs={{8,4},{9,5},{6,10},{7,11},{24,20},{25,21},{22,26},{23,27}} | collective-permute-start | bytes 3145736 | tf_op jit(solution)/shard_map/ppermute | solution.py:85
  292.4 47.9 %collective-permute-start.18 = (bf16[2048,256]{1,0:T(8,128)(2,1)S(1)}, bf16[2048,256]{1,0:T(8,128)(2,1)S(1)}, u32[]{:S(2)}, u32[]{:S(2)}) collective-permute-start(bf16[2048,256]{1,0:T(8,128)(2,1)S(1)} %add_convert_fusion.4), channel_id=1, source_target_pairs={{8,4},{9,5},{6,10},{7,11},{24,20},{25,21},{22,26},{23,27}} | collective-permute-start | bytes 3145736 | tf_op jit(solution)/shard_map/ppermute | solution.py:85
  295.0 68.4 %collective-permute-start.11 = (bf16[2048,256]{1,0:T(8,128)(2,1)S(1)}, bf16[2048,256]{1,0:T(8,128)(2,1)S(1)}, u32[]{:S(2)}, u32[]{:S(2)}) collective-permute-start(bf16[2048,256]{1,0:T(8,128)(2,1)S(1)} %copy-done.12), channel_id=1, source_target_pairs={{0,2},{4,6},{1,3},{5,7},{14,12},{10,8},{15,13},{11,9},{16,18},{20,... | collective-permute-start | bytes 3145736 | tf_op jit(solution)/shard_map/ppermute | solution.py:85
  319.3 40.8 %collective-permute-start.31 = (bf16[2048,256]{1,0:T(8,128)(2,1)S(1)}, bf16[2048,256]{1,0:T(8,128)(2,1)S(1)}, u32[]{:S(2)}, u32[]{:S(2)}) collective-permute-start(bf16[2048,256]{1,0:T(8,128)(2,1)S(1)} %add_convert_fusion.1), channel_id=1, source_target_pairs={{8,4},{9,5},{6,10},{7,11},{24,20},{25,21},{22,26},{23,27}} | collective-permute-start | bytes 3145736 | tf_op jit(solution)/shard_map/ppermute | solution.py:85
  322.4 49.5 %collective-permute-start.22 = (bf16[2048,256]{1,0:T(8,128)(2,1)S(1)}, bf16[2048,256]{1,0:T(8,128)(2,1)}, u32[]{:S(2)}, u32[]{:S(2)}) collective-permute-start(bf16[2048,256]{1,0:T(8,128)(2,1)S(1)} %copy-done.11), channel_id=1, source_target_pairs={{0,2},{4,6},{1,3},{5,7},{14,12},{10,8},{15,13},{11,9},{16,18},{20,... | collective-permute-start | bytes 3145736 | tf_op jit(solution)/shard_map/ppermute | solution.py:85
  343.6 52.1 %collective-permute-start.35 = (bf16[2048,256]{1,0:T(8,128)(2,1)}, bf16[2048,256]{1,0:T(8,128)(2,1)S(1)}, u32[]{:S(2)}, u32[]{:S(2)}) collective-permute-start(bf16[2048,256]{1,0:T(8,128)(2,1)} %fusion.16), channel_id=1, source_target_pairs={{0,2},{4,6},{1,3},{5,7},{14,12},{10,8},{15,13},{11,9},{16,18},{20,... | collective-permute-start | bytes 3145736 | tf_op jit(solution)/shard_map/ppermute | solution.py:85
  363.3 44.1 %collective-permute-start.32 = (bf16[2048,256]{1,0:T(8,128)(2,1)S(1)}, bf16[2048,256]{1,0:T(8,128)(2,1)S(1)}, u32[]{:S(2)}, u32[]{:S(2)}) collective-permute-start(bf16[2048,256]{1,0:T(8,128)(2,1)S(1)} %add_convert_fusion), channel_id=1, source_target_pairs={{4,0},{5,1},{10,14},{11,15},{20,16},{21,17},{26,30},{27,31}} | collective-permute-start | bytes 3145736 | tf_op jit(solution)/shard_map/ppermute | solution.py:85
  390.1 34.0 %collective-permute-start.36 = (f32[256,256]{1,0:T(8,128)S(1)}, f32[256,256]{1,0:T(8,128)S(1)}, u32[]{:S(2)}, u32[]{:S(2)}) collective-permute-start(f32[256,256]{1,0:T(8,128)S(1)} %fusion.61), channel_id=1, source_target_pairs={{0,4},{1,5},{2,6},{3,7},{4,0},{5,1},{6,2},{7,3},{8,12},{9,13},{10,... | collective-permute-start | bytes 786440 | tf_op jit(solution)/shard_map/ppermute | solution.py:85
  421.0 36.1 %collective-permute-start.24 = (f32[2,256,256]{2,1,0:T(8,128)S(1)}, f32[2,256,256]{2,1,0:T(8,128)S(1)}, u32[]{:S(2)}, u32[]{:S(2)}) collective-permute-start(f32[2,256,256]{2,1,0:T(8,128)S(1)} %fusion.83), channel_id=1, source_target_pairs={{0,12},{1,13},{2,14},{3,15},{4,8},{5,9},{6,10},{7,11},{8,4},{9,5},... | collective-permute-start | bytes 1572872 | tf_op jit(solution)/shard_map/ppermute | solution.py:85
  424.2 38.3 %collective-permute-start.37 = (f32[256,256]{1,0:T(8,128)S(1)}, f32[256,256]{1,0:T(8,128)S(1)}, u32[]{:S(2)}, u32[]{:S(2)}) collective-permute-start(f32[256,256]{1,0:T(8,128)S(1)} %add.135), channel_id=1, source_target_pairs={{0,12},{1,13},{2,14},{3,15},{4,8},{5,9},{6,10},{7,11},{8,4},{9,5},... | collective-permute-start | bytes 786440 | tf_op jit(solution)/shard_map/ppermute | solution.py:85
  (34 other events, 575.0 us)

commit v2 on v1

--- a/solution.py
+++ b/solution.py
@@ -161,33 +161,66 @@
     def pick(a, b):
         return jnp.where(first, a, b)
 
-    def root_product(v):
-        r1 = across(v, hops([(0, 1), (1, 2)]))
-        w = across(v, over([2, 3]))
-        q_own = mul_t(sigma_root, v)
-        d_own = across(q_own.astype(bf16), hops([(3, 2)]))
-        q_other = mul_t(other, v)
-        d_other = across(q_other.astype(bf16), hops([(3, 2)]))
-        r2 = across(r1, hops([(1, 2), (2, 3)]))
-        w_far = across(w, hops([(0, 1), (1, 0)]))
-        s_own = across((q_own + d_own).astype(bf16), hops([(2, 1)]))
-        s_other = across((q_other + d_other).astype(bf16), hops([(2, 1)]))
-        r3 = across(r2, hops([(2, 3)]))
-        w0 = jnp.where(step == 0, w, w_far)
-        w1 = jnp.where(step == 0, w_far, w)
-        g = mul(sigma_root, pick(w0, w1)) + mul(other, pick(w1, w0))
-        g = across(g.astype(bf16), over([0, 1]))
-        f0 = pick(s_own, s_other) + pick(q_own, q_other)
-        f0 = across(f0.astype(bf16), hops([(1, 0)]))
-        a = jnp.where(step == 0, v, jnp.where(step == 1, r1, jnp.where(step == 2, r2, r3)))
-        b = jnp.where(step == 1, v, jnp.where(step == 2, r1, jnp.where(step == 3, r2, 0)))
-        x = mul(sigma_root, pick(a, b)) + mul(other, pick(b, a))
-        rest = jnp.where(step == 0, f0, jnp.where(step == 1, pick(s_other, s_own), g))
-        return x + rest
+    def cut(wide, count):
+        return [wide[:, p * block : (p + 1) * block] for p in range(count)]
+
+    def wide(parts):
+        return parts[0] if len(parts) == 1 else jnp.concatenate(parts, axis=1)
+
+    def add(*parts):
+        return sum(p.astype(jnp.float32) for p in parts)
+
+    def root_products(v, groups):
+        n = len(v)
+        last = n - 1
+        q_own = mul_t(sigma_root, wide(v)).astype(bf16)
+        q_own = cut(q_own, n)
+        r1 = [across(p, hops([(0, 1), (1, 2)])) for p in v]
+        d_own = [across(p, hops([(3, 2)])) for p in q_own]
+        w = [across(p, over([2, 3])) for p in v]
+        held, r1[0] = lax.optimization_barrier((other, r1[0]))
+        q_other = mul_t(held, wide(v)).astype(bf16)
+        q_other, r1[last] = lax.optimization_barrier((q_other, r1[last]))
+        q_other = cut(q_other, n)
+        d_other = [across(p, hops([(3, 2)])) for p in q_other]
+        s_own = [across(add(p, d).astype(bf16), hops([(2, 1)])) for p, d in zip(q_own, d_own)]
+        r2 = [across(p, hops([(1, 2), (2, 3)])) for p in r1]
+        w_far = [across(p, hops([(0, 1), (1, 0)])) for p in w]
+        s_other = [across(add(p, d).astype(bf16), hops([(2, 1)])) for p, d in zip(q_other, d_other)]
+        w0 = [jnp.where(step == 0, p, far) for p, far in zip(w, w_far)]
+        w1 = [jnp.where(step == 0, far, p) for p, far in zip(w, w_far)]
+        g = mul(sigma_root, wide([pick(p, q) for p, q in zip(w0, w1)]))
+        g = (g + mul(held, wide([pick(q, p) for p, q in zip(w0, w1)]))).astype(bf16)
+        g, r2[last] = lax.optimization_barrier((g, r2[last]))
+        g = [across(p, over([0, 1])) for p in cut(g, n)]
+        r3 = [across(p, hops([(2, 3)])) for p in r2]
+        f0 = [
+            across(add(pick(s_own[p], s_other[p]), pick(q_own[p], q_other[p])).astype(bf16), hops([(1, 0)]))
+            for p in range(n)
+        ]
+        result, start = [], 0
+        for size in groups:
+            here = range(start, start + size)
+            a, b, rest = [], [], []
+            for p in here:
+                x0 = jnp.where(step == 2, r2[p], r3[p])
+                x0 = jnp.where(step == 0, v[p], jnp.where(step == 1, r1[p], x0))
+                x1 = jnp.where(step == 2, r1[p], jnp.where(step == 3, r2[p], 0))
+                x1 = jnp.where(step == 1, v[p], x1)
+                a.append(pick(x0, x1))
+                b.append(pick(x1, x0))
+                late = jnp.where(step == 1, pick(s_other[p], s_own[p]), g[p])
+                rest.append(jnp.where(step == 0, f0[p], late))
+            result.append(mul(sigma_root, wide(a)) + mul(held, wide(b)) + wide(rest))
+            start += size
+        return result
 
     u1 = panels(lower1, mask1, inv1)
     u2 = panels(lower2, mask2, inv2)
-    off1 = [(-root_product(u)).astype(bf16) for u in u1]
+    x1, x2 = root_products(u1 + u2, (count1, count2))
+    off1_wide = (-x1).astype(bf16)
+    off1 = cut(off1_wide, count1)
+    x2 = cut(x2, count2)
     term1 = sum_rows(jnp.stack([mul_t(u, o) for u, o in zip(u1, off1)]))
     base1 = jnp.stack([mul_t(inv1[p], inv1[p]) for p in range(count1)])
     diag1 = (base1 - term1).astype(bf16)
@@ -203,13 +236,13 @@
         cross = sum_rows(mul_t(par_off, u2[k]))
         par = (-(cross + mul(par_diag, link_u))).astype(bf16)
         known = mul_t(inv2[k], inv2[k]) - mul_t(link_u, par)
-        o2 = (-(root_product(u2[k]) + mul(par_off, link_u))).astype(bf16)
+        o2 = (-(x2[k] + mul(par_off, link_u))).astype(bf16)
         pair = sum_rows(mul_t(u2[k], o2))
         off2.append(o2)
         par2.append(par)
         diag2.append((known - pair).astype(bf16))
     return (
-        jnp.concatenate(off1, axis=1),
+        off1_wide,
         diag1,
         jnp.concatenate(off2, axis=1),
         jnp.stack(par2),

time: 475 us -> 477 us (level)
  starting transfers between devices: 110 us -> 156 us
  matrix products: 135 us -> 94.9 us
  waiting for transfers between devices: 200 us -> 175 us
  other arithmetic: 17.5 us -> 28.9 us
  local copies, waits for them, and re-layouts: 1.75 us -> 11 us
    ppermute x40, starting transfers between devices: 110 us -> 156 us  [across(): return lax.ppermute(value, ('row', 'col'), pairs)]
    ppermute x40, waiting for transfers between devices: 200 us -> 175 us  [across(): return lax.ppermute(value, ('row', 'col'), pairs)]
    dot_general x14 -> x10, matrix products: 51.8 us -> 30 us  [mul_t(): lax.dot_general(a, b, (((0,), (0,)), ((), ())), preferred_element_type=jn...]
    dot_general x18 -> x12, matrix products: 83.2 us -> 64.9 us  [mul(): return jnp.dot(a, b, preferred_element_type=jnp.float32)]
    select_n x3 -> x10, other arithmetic: 3.46 us -> 16 us  [the longest x7 13.6 us: pick(): return jnp.where(first, a, b)]
    unnamed x57 -> x35, local copies, waits for them, and re-layouts: 1.16 us -> 6.61 us
    convert_element_type x9 -> x3, other arithmetic: 10.6 us -> 8.24 us  [the longest x2 5.77 us: root_products(): add(p, d).astype(bf16)]
  transfers between devices with their start and end apart: 40 -> 40, of which waited for: 16 -> 14; matrix products, arithmetic and copies ran while one was open for 33% -> 28% of each run, Pallas kernels for 0% -> 0%
where the time goes in v2:
time: 477 us; the launch traced here: 468 us
  waiting for transfers between devices  175 us (37%)
  starting transfers between devices  156 us (33%)
  matrix products  94.9 us (20%)
  other arithmetic  28.9 us (6%)
  local copies, waits for them, and re-layouts  11 us (2%)
    ppermute x40, waiting for transfers between devices, across(): return lax.ppermute(value, ('row', 'col'), pairs)  175 us
    ppermute x40, starting transfers between devices, across(): return lax.ppermute(value, ('row', 'col'), pairs)  156 us
    dot_general x12, matrix products, mul(): return jnp.dot(a, b, preferred_element_type=jnp.float32)  64.9 us
    dot_general x10, matrix products, mul_t(): lax.dot_general(a, b, (((0,), (0,)), ((), ())), preferred_element_type=jn...  30 us
    select_n x7, other arithmetic, pick(): return jnp.where(first, a, b)  13.6 us
  transfers between devices with their start and end apart: 40, of which 14 were waited for; matrix products, arithmetic and copies ran while one was open for 28% of the time, Pallas kernels for 0%

profile of v2, /device:TPU:10, one launch (start us, length us, event | category | flops | bytes accessed | tf_op | source)
XLA Modules:
  0.0 468.3 jit_solution(18310877821409344290)
XLA Ops:
  1.7 2.8 convolution_convert_fusion.4
  5.8 2.9 convolution_convert_fusion.3
  12.4 10.0 %fusion.15 = bf16[2048,768]{0,1:T(8,128)(2,1)S(1)} fusion(bf16[2048,2048]{1,0:T(8,128)(2,1)} %param.9, bf16[2048,256]{0,1:T(8,128)(2,1)} %convolution_convert_fusion.2, bf16[2048,256]{0,1:T(8,128)(2,1)} %convolution_convert_fusion.3, bf16[2048,256]{0,1:T(8,128)(2,1)} %convolution_convert_fusion.4), kind=kOutput, calls=%fused_computation.20 | convolution fusion | flops 6453460992 | bytes 14680064 | tf_op jit(solution)/shard_map/dot_general | solution.py:133
  27.5 5.2 %collective-permute-done.13 = bf16[2048,256]{0,1:T(8,128)(2,1)} collective-permute-done((bf16[2048,256]{0,1:T(8,128)(2,1)}, bf16[2048,256]{0,1:T(8,128)(2,1)}, u32[]{:S(2)}, u32[]{:S(2)}) %collective-permute-start.13) | collective-permute-done | bytes 1048608 | tf_op jit(solution)/shard_map/ppermute | solution.py:85
  34.4 20.3 %collective-permute-done.15 = bf16[2048,256]{0,1:T(8,128)(2,1)} collective-permute-done((bf16[2048,256]{0,1:T(8,128)(2,1)}, bf16[2048,256]{0,1:T(8,128)(2,1)}, u32[]{:S(2)}, u32[]{:S(2)}) %collective-permute-start.15) | collective-permute-done | bytes 1048608 | tf_op jit(solution)/shard_map/ppermute | solution.py:85
  59.9 22.3 %collective-permute-start.4 = (bf16[2048,256]{0,1:T(8,128)(2,1)}, bf16[2048,256]{0,1:T(8,128)(2,1)S(1)}, u32[]{:S(2)}, u32[]{:S(2)}) collective-permute-start(bf16[2048,256]{0,1:T(8,128)(2,1)} %convolution_convert_fusion.3), channel_id=1, source_target_pairs={{0,4},{4,8},{1,5},{5,9},{14,10},{10,6},{15,11},{11,7},{16,20},{20,... | collective-permute-start | bytes 3145736 | tf_op jit(solution)/shard_map/ppermute | solution.py:85
  84.1 3.3 add_convert_fusion.2
  87.4 20.5 %collective-permute-start.1 = (bf16[2048,256]{0,1:T(8,128)(2,1)}, bf16[2048,256]{0,1:T(8,128)(2,1)}, u32[]{:S(2)}, u32[]{:S(2)}) collective-permute-start(bf16[2048,256]{0,1:T(8,128)(2,1)} %convolution_convert_fusion.4), channel_id=1, source_target_pairs={{0,4},{4,8},{1,5},{5,9},{14,10},{10,6},{15,11},{11,7},{16,20},{20,... | collective-permute-start | bytes 3145736 | tf_op jit(solution)/shard_map/ppermute | solution.py:85
  109.8 2.7 broadcast_select_fusion.12
  114.4 14.7 %collective-permute-done.16 = bf16[2048,256]{0,1:T(8,128)(2,1)S(1)} collective-permute-done((bf16[2048,256]{0,1:T(8,128)(2,1)}, bf16[2048,256]{0,1:T(8,128)(2,1)S(1)}, u32[]{:S(2)}, u32[]{:S(2)}) %collective-permute-start.16) | collective-permute-done | bytes 1048608 | tf_op jit(solution)/shard_map/ppermute | solution.py:85
  133.0 41.1 %collective-permute-done.18 = bf16[2048,256]{0,1:T(8,128)(2,1)S(1)} collective-permute-done((bf16[2048,256]{0,1:T(8,128)(2,1)}, bf16[2048,256]{0,1:T(8,128)(2,1)S(1)}, u32[]{:S(2)}, u32[]{:S(2)}) %collective-permute-start.18) | collective-permute-done | bytes 1048608 | tf_op jit(solution)/shard_map/ppermute | solution.py:85
  179.9 10.0 %convolution_convert_fusion = bf16[2048,768]{0,1:T(8,128)(2,1)S(1)} fusion(bf16[2048,2048]{1,0:T(8,128)(2,1)} %collective-permute-done, bf16[2048,256]{0,1:T(8,128)(2,1)} %convolution_convert_fusion.2, bf16[2048,256]{0,1:T(8,128)(2,1)} %convolution_convert_fusion.3, bf16[2048,256]{0,1:T(8,128)(2,1)} %convolution_convert_fusion.4), kind=kOutput, calls=%fused_computation.6 | convolution fusion | flops 6453460992 | bytes 14680064 | tf_op jit(solution)/shard_map/dot_general | solution.py:133
  189.9 5.2 %collective-permute-done.9 = bf16[2048,256]{0,1:T(8,128)(2,1)S(1)} collective-permute-done((bf16[2048,256]{0,1:T(8,128)(2,1)}, bf16[2048,256]{0,1:T(8,128)(2,1)S(1)}, u32[]{:S(2)}, u32[]{:S(2)}) %collective-permute-start.9) | collective-permute-done | bytes 1048608 | tf_op jit(solution)/shard_map/ppermute | solution.py:85
  200.1 9.6 %collective-permute-start.19 = (bf16[2048,256]{0,1:T(8,128)(2,1)S(1)}, bf16[2048,256]{0,1:T(8,128)(2,1)}, u32[]{:S(2)}, u32[]{:S(2)}) collective-permute-start(bf16[2048,256]{0,1:T(8,128)(2,1)S(1)} %collective-permute-done.9), channel_id=1, source_target_pairs={{4,8},{8,12},{5,9},{9,13},{10,6},{6,2},{11,7},{7,3},{20,24},{24,28... | collective-permute-start | bytes 3145736 | tf_op jit(solution)/shard_map/ppermute | solution.py:85
  211.2 10.9 %fusion.9 = f32[2048,768]{0,1:T(8,128)} fusion(bf16[2048,2048]{1,0:T(8,128)(2,1)} %collective-permute-done, bf16[2048,256]{0,1:T(8,128)(2,1)S(1)} %get-tuple-element.53, bf16[2048,256]{0,1:T(8,128)(2,1)S(1)} %get-tuple-element.51, bf16[2048,256]{0,1:T(8,128)(2,1)S(1)} %get-tuple-element.49), kind=kOutput, calls=%fused_computation.14 | convolution fusion | flops 6451888128 | bytes 17825792 | tf_op jit(solution)/shard_map/dot_general | solution.py:129
  223.4 42.2 %collective-permute-start.2 = (bf16[2048,256]{0,1:T(8,128)(2,1)}, bf16[2048,256]{0,1:T(8,128)(2,1)}, u32[]{:S(2)}, u32[]{:S(2)}) collective-permute-start(bf16[2048,256]{0,1:T(8,128)(2,1)} %collective-permute-done.1), channel_id=1, source_target_pairs={{4,8},{8,12},{5,9},{9,13},{10,6},{6,2},{11,7},{7,3},{20,24},{24,28... | collective-permute-start | bytes 3145736 | tf_op jit(solution)/shard_map/ppermute | solution.py:85
  272.0 11.0 %fusion = bf16[2048,768]{0,1:T(8,128)(2,1)S(1)} fusion(f32[2048,768]{0,1:T(8,128)} %fusion.9, bf16[2048,2048]{1,0:T(8,128)(2,1)} %param.9, bf16[2048,256]{0,1:T(8,128)(2,1)} %get-tuple-element.52, bf16[2048,256]{0,1:T(8,128)(2,1)} %get-tuple-element.50, bf16[2048,256]{0,1:T(8,128)(2,1)} %get-tuple-element.48), kind=kOutput, calls=%fused_computation.1 | convolution fusion | flops 6455033856 | bytes 20971520 | tf_op jit(solution)/shard_map/dot_general | solution.py:129
  286.8 9.4 %collective-permute-done.11 = bf16[2048,256]{0,1:T(8,128)(2,1)S(1)} collective-permute-done((bf16[2048,256]{0,1:T(8,128)(2,1)}, bf16[2048,256]{0,1:T(8,128)(2,1)S(1)}, u32[]{:S(2)}, u32[]{:S(2)}) %collective-permute-start.11) | collective-permute-done | bytes 1048608 | tf_op jit(solution)/shard_map/ppermute | solution.py:85
  299.0 19.8 %collective-permute-done.24 = bf16[2048,256]{0,1:T(8,128)(2,1)S(1)} collective-permute-done((bf16[2048,256]{0,1:T(8,128)(2,1)}, bf16[2048,256]{0,1:T(8,128)(2,1)S(1)}, u32[]{:S(2)}, u32[]{:S(2)}) %collective-permute-start.24) | collective-permute-done | bytes 1048608 | tf_op jit(solution)/shard_map/ppermute | solution.py:85
  321.4 14.6 %collective-permute-done.33 = bf16[2048,256]{0,1:T(8,128)(2,1)S(1)} collective-permute-done((bf16[2048,256]{0,1:T(8,128)(2,1)}, bf16[2048,256]{0,1:T(8,128)(2,1)S(1)}, u32[]{:S(2)}, u32[]{:S(2)}) %collective-permute-start.33) | collective-permute-done | bytes 1048608 | tf_op jit(solution)/shard_map/ppermute | solution.py:85
  336.1 3.6 collective-permute-start.35
  342.2 12.2 %collective-permute-start.12 = (bf16[2048,256]{0,1:T(8,128)(2,1)S(1)}, bf16[2048,256]{0,1:T(8,128)(2,1)S(1)}, u32[]{:S(2)}, u32[]{:S(2)}) collective-permute-start(bf16[2048,256]{0,1:T(8,128)(2,1)S(1)} %get-tuple-element.29), channel_id=1, source_target_pairs={{4,0},{5,1},{10,14},{11,15},{20,16},{21,17},{26,30},{27,31}} | collective-permute-start | bytes 3145736 | tf_op jit(solution)/shard_map/ppermute | solution.py:85
  357.7 9.9 %fusion.21 = f32[512,2048]{1,0:T(8,128)} fusion(bf16[2048,2048]{1,0:T(8,128)(2,1)} %param.9, bf16[2048,256]{0,1:T(8,128)(2,1)S(1)} %copy-done.3, bf16[2048,256]{0,1:T(8,128)(2,1)S(1)} %broadcast_select_fusion.16), kind=kOutput, calls=%fused_computation.30 | convolution fusion | flops 4299161600 | bytes 14680064 | tf_op jit(solution)/shard_map/dot_general | solution.py:129
  370.9 7.2 %fusion.31 = f32[2048,256]{0,1:T(8,128)} fusion(bf16[2048,2048]{1,0:T(8,128)(2,1)} %collective-permute-done, bf16[2048,256]{0,1:T(8,128)(2,1)S(1)} %get-tuple-element.47, bf16[2048,256]{0,1:T(8,128)(2,1)S(1)} %get-tuple-element.46, pred[]{:T(512)S(6)} %eq.16), kind=kOutput, calls=%fused_computation.55 | convolution fusion | flops 2148007936 | bytes 12582913 | tf_op jit(solution)/shard_map/dot_general | solution.py:129
  379.6 12.9 %collective-permute-done.25 = bf16[2048,256]{0,1:T(8,128)(2,1)S(1)} collective-permute-done((bf16[2048,256]{0,1:T(8,128)(2,1)S(1)}, bf16[2048,256]{0,1:T(8,128)(2,1)S(1)}, u32[]{:S(2)}, u32[]{:S(2)}) %collective-permute-start.25) | collective-permute-done | bytes 1048608 | tf_op jit(solution)/shard_map/ppermute | solution.py:85
  392.9 10.4 %fusion.3 = bf16[2048,512]{0,1:T(8,128)(2,1)S(1)} fusion(f32[512,2048]{1,0:T(8,128)} %fusion.21, bf16[2048,2048]{1,0:T(8,128)(2,1)} %collective-permute-done, bf16[2048,256]{0,1:T(8,128)(2,1)S(1)} %copy-done.7, bf16[2048,256]{0,1:T(8,128)(2,1)S(1)} %get-tuple-element.22, bf16[2048,256]{0,1:T(8,128)(2,1)S(1)} %select_select_fusion.2, ...), kind=kOutput, calls=%fused_computation.5 | convolution fusion | flops 4307550208 | bytes 18874368 | tf_op jit(solution)/shard_map/dot_general | solution.py:129
  410.7 3.9 collective-permute-done.34
  414.5 6.4 %fusion.20 = bf16[2048,256]{0,1:T(8,128)(2,1)S(1)} fusion(f32[2048,256]{0,1:T(8,128)S(1)} %fusion.48, f32[2048,256]{0,1:T(8,128)S(1)} %copy-done.13, bf16[2048,2048]{1,0:T(8,128)(2,1)} %param.9, bf16[2048,256]{0,1:T(8,128)(2,1)S(1)} %collective-permute-done.34, bf16[2048,256]{0,1:T(8,128)(2,1)} %collective-permute-done.35, ...), kind=kOutput, calls=%fused_computation.26 | convolution fusion | flops 2152726528 | bytes 19922948 | tf_op jit(solution)/shard_map/dot_general | solution.py:129
  422.8 3.7 collective-permute-done.27
  432.8 16.7 %collective-permute-done.36 = f32[256,256]{1,0:T(8,128)S(1)} collective-permute-done((f32[256,256]{1,0:T(8,128)S(1)}, f32[256,256]{1,0:T(8,128)S(1)}, u32[]{:S(2)}, u32[]{:S(2)}) %collective-permute-start.36) | collective-permute-done | bytes 262176 | tf_op jit(solution)/shard_map/ppermute | solution.py:85
  453.0 4.0 copy.19
  460.6 6.6 %collective-permute-done.39 = f32[256,256]{1,0:T(8,128)S(1)} collective-permute-done((f32[256,256]{1,0:T(8,128)S(1)}, f32[256,256]{1,0:T(8,128)S(1)}, u32[]{:S(2)}, u32[]{:S(2)}) %collective-permute-start.39) | collective-permute-done | bytes 262176 | tf_op jit(solution)/shard_map/ppermute | solution.py:85
  (130 shorter events, 90.3 us)
Async XLA Ops:
  0.7 179.3 %collective-permute-start = (bf16[2048,2048]{1,0:T(8,128)(2,1)}, bf16[2048,2048]{1,0:T(8,128)(2,1)}, u32[]{:S(2)}, u32[]{:S(2)}) collective-permute-start(bf16[2048,2048]{1,0:T(8,128)(2,1)} %param.9), channel_id=1, source_target_pairs={{0,1},{4,5},{8,9},{12,13},{1,0},{5,4},{9,8},{13,12},{14,15},{10,11... | collective-permute-start | bytes 25165832 | tf_op jit(solution)/shard_map/ppermute | solution.py:85
  4.5 28.2 %collective-permute-start.13 = (bf16[2048,256]{0,1:T(8,128)(2,1)}, bf16[2048,256]{0,1:T(8,128)(2,1)}, u32[]{:S(2)}, u32[]{:S(2)}) collective-permute-start(bf16[2048,256]{0,1:T(8,128)(2,1)} %convolution_convert_fusion.4), channel_id=1, source_target_pairs={{8,10},{12,14},{9,11},{13,15},{6,4},{2,0},{7,5},{3,1},{24,26},{28,... | collective-permute-start | bytes 3145736 | tf_op jit(solution)/shard_map/ppermute | solution.py:85
  8.7 46.0 %collective-permute-start.15 = (bf16[2048,256]{0,1:T(8,128)(2,1)}, bf16[2048,256]{0,1:T(8,128)(2,1)}, u32[]{:S(2)}, u32[]{:S(2)}) collective-permute-start(bf16[2048,256]{0,1:T(8,128)(2,1)} %convolution_convert_fusion.3), channel_id=1, source_target_pairs={{8,10},{12,14},{9,11},{13,15},{6,4},{2,0},{7,5},{3,1},{24,26},{28,... | collective-permute-start | bytes 3145736 | tf_op jit(solution)/shard_map/ppermute | solution.py:85
  24.2 31.8 %collective-permute-start.21 = (bf16[2048,256]{0,1:T(8,128)(2,1)S(1)}, bf16[2048,256]{0,1:T(8,128)(2,1)}, u32[]{:S(2)}, u32[]{:S(2)}) collective-permute-start(bf16[2048,256]{0,1:T(8,128)(2,1)S(1)} %get-tuple-element.44), channel_id=1, source_target_pairs={{12,8},{13,9},{2,6},{3,7},{28,24},{29,25},{18,22},{19,23}} | collective-permute-start | bytes 3145736 | tf_op jit(solution)/shard_map/ppermute | solution.py:85
  25.8 34.0 %collective-permute-start.30 = (bf16[2048,256]{0,1:T(8,128)(2,1)}, bf16[2048,256]{0,1:T(8,128)(2,1)}, u32[]{:S(2)}, u32[]{:S(2)}) collective-permute-start(bf16[2048,256]{0,1:T(8,128)(2,1)} %get-tuple-element.43), channel_id=1, source_target_pairs={{12,8},{13,9},{2,6},{3,7},{28,24},{29,25},{18,22},{19,23}} | collective-permute-start | bytes 3145736 | tf_op jit(solution)/shard_map/ppermute | solution.py:85
  32.7 49.5 %collective-permute-start.7 = (bf16[2048,256]{0,1:T(8,128)(2,1)}, bf16[2048,256]{0,1:T(8,128)(2,1)}, u32[]{:S(2)}, u32[]{:S(2)}) collective-permute-start(bf16[2048,256]{0,1:T(8,128)(2,1)} %get-tuple-element.45), channel_id=1, source_target_pairs={{12,8},{13,9},{2,6},{3,7},{28,24},{29,25},{18,22},{19,23}} | collective-permute-start | bytes 3145736 | tf_op jit(solution)/shard_map/ppermute | solution.py:85
  54.7 32.7 %collective-permute-start.17 = (bf16[2048,256]{0,1:T(8,128)(2,1)}, bf16[2048,256]{0,1:T(8,128)(2,1)}, u32[]{:S(2)}, u32[]{:S(2)}) collective-permute-start(bf16[2048,256]{0,1:T(8,128)(2,1)} %convolution_convert_fusion.2), channel_id=1, source_target_pairs={{8,10},{12,14},{9,11},{13,15},{6,4},{2,0},{7,5},{3,1},{24,26},{28,... | collective-permute-start | bytes 3145736 | tf_op jit(solution)/shard_map/ppermute | solution.py:85
  56.0 51.9 %collective-permute-start.14 = (bf16[2048,256]{0,1:T(8,128)(2,1)}, bf16[2048,256]{0,1:T(8,128)(2,1)}, u32[]{:S(2)}, u32[]{:S(2)}) collective-permute-start(bf16[2048,256]{0,1:T(8,128)(2,1)} %collective-permute-done.13), channel_id=1, source_target_pairs={{0,4},{4,0},{1,5},{5,1},{14,10},{10,14},{15,11},{11,15},{16,20},{2... | collective-permute-start | bytes 3145736 | tf_op jit(solution)/shard_map/ppermute | solution.py:85
  59.9 52.6 %collective-permute-start.4 = (bf16[2048,256]{0,1:T(8,128)(2,1)}, bf16[2048,256]{0,1:T(8,128)(2,1)S(1)}, u32[]{:S(2)}, u32[]{:S(2)}) collective-permute-start(bf16[2048,256]{0,1:T(8,128)(2,1)} %convolution_convert_fusion.3), channel_id=1, source_target_pairs={{0,4},{4,8},{1,5},{5,9},{14,10},{10,6},{15,11},{11,7},{16,20},{20,... | collective-permute-start | bytes 3145736 | tf_op jit(solution)/shard_map/ppermute | solution.py:85
  82.2 47.0 %collective-permute-start.16 = (bf16[2048,256]{0,1:T(8,128)(2,1)}, bf16[2048,256]{0,1:T(8,128)(2,1)S(1)}, u32[]{:S(2)}, u32[]{:S(2)}) collective-permute-start(bf16[2048,256]{0,1:T(8,128)(2,1)} %collective-permute-done.15), channel_id=1, source_target_pairs={{0,4},{4,0},{1,5},{5,1},{14,10},{10,14},{15,11},{11,15},{16,20},{2... | collective-permute-start | bytes 3145736 | tf_op jit(solution)/shard_map/ppermute | solution.py:85
  87.4 90.5 %collective-permute-start.1 = (bf16[2048,256]{0,1:T(8,128)(2,1)}, bf16[2048,256]{0,1:T(8,128)(2,1)}, u32[]{:S(2)}, u32[]{:S(2)}) collective-permute-start(bf16[2048,256]{0,1:T(8,128)(2,1)} %convolution_convert_fusion.4), channel_id=1, source_target_pairs={{0,4},{4,8},{1,5},{5,9},{14,10},{10,6},{15,11},{11,7},{16,20},{20,... | collective-permute-start | bytes 3145736 | tf_op jit(solution)/shard_map/ppermute | solution.py:85
  107.9 66.2 %collective-permute-start.18 = (bf16[2048,256]{0,1:T(8,128)(2,1)}, bf16[2048,256]{0,1:T(8,128)(2,1)S(1)}, u32[]{:S(2)}, u32[]{:S(2)}) collective-permute-start(bf16[2048,256]{0,1:T(8,128)(2,1)} %collective-permute-done.17), channel_id=1, source_target_pairs={{0,4},{4,0},{1,5},{5,1},{14,10},{10,14},{15,11},{11,15},{16,20},{2... | collective-permute-start | bytes 3145736 | tf_op jit(solution)/shard_map/ppermute | solution.py:85
  112.5 82.6 %collective-permute-start.9 = (bf16[2048,256]{0,1:T(8,128)(2,1)}, bf16[2048,256]{0,1:T(8,128)(2,1)S(1)}, u32[]{:S(2)}, u32[]{:S(2)}) collective-permute-start(bf16[2048,256]{0,1:T(8,128)(2,1)} %convolution_convert_fusion.2), channel_id=1, source_target_pairs={{0,4},{4,8},{1,5},{5,9},{14,10},{10,6},{15,11},{11,7},{16,20},{20,... | collective-permute-start | bytes 3145736 | tf_op jit(solution)/shard_map/ppermute | solution.py:85
  129.1 50.1 %collective-permute-start.5 = (bf16[2048,256]{0,1:T(8,128)(2,1)S(1)}, bf16[2048,256]{0,1:T(8,128)(2,1)S(1)}, u32[]{:S(2)}, u32[]{:S(2)}) collective-permute-start(bf16[2048,256]{0,1:T(8,128)(2,1)S(1)} %collective-permute-done.4), channel_id=1, source_target_pairs={{4,8},{8,12},{5,9},{9,13},{10,6},{6,2},{11,7},{7,3},{20,24},{24,28... | collective-permute-start | bytes 3145736 | tf_op jit(solution)/shard_map/ppermute | solution.py:85
  174.0 94.0 %collective-permute-start.22 = (bf16[2048,256]{0,1:T(8,128)(2,1)S(1)}, bf16[2048,256]{0,1:T(8,128)(2,1)S(1)}, u32[]{:S(2)}, u32[]{:S(2)}) collective-permute-start(bf16[2048,256]{0,1:T(8,128)(2,1)S(1)} %get-tuple-element.42), channel_id=1, source_target_pairs={{8,4},{9,5},{6,10},{7,11},{24,20},{25,21},{22,26},{23,27}} | collective-permute-start | bytes 3145736 | tf_op jit(solution)/shard_map/ppermute | solution.py:85
  177.9 91.5 %collective-permute-start.31 = (bf16[2048,256]{0,1:T(8,128)(2,1)S(1)}, bf16[2048,256]{0,1:T(8,128)(2,1)S(1)}, u32[]{:S(2)}, u32[]{:S(2)}) collective-permute-start(bf16[2048,256]{0,1:T(8,128)(2,1)S(1)} %get-tuple-element.40), channel_id=1, source_target_pairs={{8,4},{9,5},{6,10},{7,11},{24,20},{25,21},{22,26},{23,27}} | collective-permute-start | bytes 3145736 | tf_op jit(solution)/shard_map/ppermute | solution.py:85
  200.1 70.5 %collective-permute-start.19 = (bf16[2048,256]{0,1:T(8,128)(2,1)S(1)}, bf16[2048,256]{0,1:T(8,128)(2,1)}, u32[]{:S(2)}, u32[]{:S(2)}) collective-permute-start(bf16[2048,256]{0,1:T(8,128)(2,1)S(1)} %collective-permute-done.9), channel_id=1, source_target_pairs={{4,8},{8,12},{5,9},{9,13},{10,6},{6,2},{11,7},{7,3},{20,24},{24,28... | collective-permute-start | bytes 3145736 | tf_op jit(solution)/shard_map/ppermute | solution.py:85
  222.1 64.0 %collective-permute-start.8 = (bf16[2048,256]{0,1:T(8,128)(2,1)S(1)}, bf16[2048,256]{0,1:T(8,128)(2,1)S(1)}, u32[]{:S(2)}, u32[]{:S(2)}) collective-permute-start(bf16[2048,256]{0,1:T(8,128)(2,1)S(1)} %get-tuple-element.41), channel_id=1, source_target_pairs={{8,4},{9,5},{6,10},{7,11},{24,20},{25,21},{22,26},{23,27}} | collective-permute-start | bytes 3145736 | tf_op jit(solution)/shard_map/ppermute | solution.py:85
  223.4 60.3 %collective-permute-start.2 = (bf16[2048,256]{0,1:T(8,128)(2,1)}, bf16[2048,256]{0,1:T(8,128)(2,1)}, u32[]{:S(2)}, u32[]{:S(2)}) collective-permute-start(bf16[2048,256]{0,1:T(8,128)(2,1)} %collective-permute-done.1), channel_id=1, source_target_pairs={{4,8},{8,12},{5,9},{9,13},{10,6},{6,2},{11,7},{7,3},{20,24},{24,28... | collective-permute-start | bytes 3145736 | tf_op jit(solution)/shard_map/ppermute | solution.py:85
  268.1 28.2 %collective-permute-start.11 = (bf16[2048,256]{0,1:T(8,128)(2,1)}, bf16[2048,256]{0,1:T(8,128)(2,1)S(1)}, u32[]{:S(2)}, u32[]{:S(2)}) collective-permute-start(bf16[2048,256]{0,1:T(8,128)(2,1)} %get-tuple-element.35), channel_id=1, source_target_pairs={{8,4},{9,5},{6,10},{7,11},{24,20},{25,21},{22,26},{23,27}} | collective-permute-start | bytes 3145736 | tf_op jit(solution)/shard_map/ppermute | solution.py:85
  269.4 49.4 %collective-permute-start.24 = (bf16[2048,256]{0,1:T(8,128)(2,1)}, bf16[2048,256]{0,1:T(8,128)(2,1)S(1)}, u32[]{:S(2)}, u32[]{:S(2)}) collective-permute-start(bf16[2048,256]{0,1:T(8,128)(2,1)} %get-tuple-element.36), channel_id=1, source_target_pairs={{8,4},{9,5},{6,10},{7,11},{24,20},{25,21},{22,26},{23,27}} | collective-permute-start | bytes 3145736 | tf_op jit(solution)/shard_map/ppermute | solution.py:85
  270.7 65.4 %collective-permute-start.33 = (bf16[2048,256]{0,1:T(8,128)(2,1)}, bf16[2048,256]{0,1:T(8,128)(2,1)S(1)}, u32[]{:S(2)}, u32[]{:S(2)}) collective-permute-start(bf16[2048,256]{0,1:T(8,128)(2,1)} %get-tuple-element.34), channel_id=1, source_target_pairs={{8,4},{9,5},{6,10},{7,11},{24,20},{25,21},{22,26},{23,27}} | collective-permute-start | bytes 3145736 | tf_op jit(solution)/shard_map/ppermute | solution.py:85
  283.6 58.5 %collective-permute-start.3 = (bf16[2048,256]{0,1:T(8,128)(2,1)}, bf16[2048,256]{0,1:T(8,128)(2,1)S(1)}, u32[]{:S(2)}, u32[]{:S(2)}) collective-permute-start(bf16[2048,256]{0,1:T(8,128)(2,1)} %collective-permute-done.2), channel_id=1, source_target_pairs={{8,12},{9,13},{6,2},{7,3},{24,28},{25,29},{22,18},{23,19}} | collective-permute-start | bytes 3145736 | tf_op jit(solution)/shard_map/ppermute | solution.py:85
  286.1 81.5 %collective-permute-start.29 = (bf16[2048,256]{0,1:T(8,128)(2,1)}, bf16[2048,256]{0,1:T(8,128)(2,1)S(1)}, u32[]{:S(2)}, u32[]{:S(2)}) collective-permute-start(bf16[2048,256]{0,1:T(8,128)(2,1)} %collective-permute-done.19), channel_id=1, source_target_pairs={{8,12},{9,13},{6,2},{7,3},{24,28},{25,29},{22,18},{23,19}} | collective-permute-start | bytes 3145736 | tf_op jit(solution)/shard_map/ppermute | solution.py:85
  296.3 81.8 %collective-permute-start.20 = (bf16[2048,256]{0,1:T(8,128)(2,1)}, bf16[2048,256]{0,1:T(8,128)(2,1)S(1)}, u32[]{:S(2)}, u32[]{:S(2)}) collective-permute-start(bf16[2048,256]{0,1:T(8,128)(2,1)} %get-tuple-element.33), channel_id=1, source_target_pairs={{0,2},{4,6},{1,3},{5,7},{14,12},{10,8},{15,13},{11,9},{16,18},{20,... | collective-permute-start | bytes 3145736 | tf_op jit(solution)/shard_map/ppermute | solution.py:85
  318.7 60.9 %collective-permute-start.26 = (bf16[2048,256]{0,1:T(8,128)(2,1)}, bf16[2048,256]{0,1:T(8,128)(2,1)S(1)}, u32[]{:S(2)}, u32[]{:S(2)}) collective-permute-start(bf16[2048,256]{0,1:T(8,128)(2,1)} %get-tuple-element.32), channel_id=1, source_target_pairs={{0,2},{4,6},{1,3},{5,7},{14,12},{10,8},{15,13},{11,9},{16,18},{20,... | collective-permute-start | bytes 3145736 | tf_op jit(solution)/shard_map/ppermute | solution.py:85
  336.1 74.6 %collective-permute-start.35 = (bf16[2048,256]{0,1:T(8,128)(2,1)}, bf16[2048,256]{0,1:T(8,128)(2,1)}, u32[]{:S(2)}, u32[]{:S(2)}) collective-permute-start(bf16[2048,256]{0,1:T(8,128)(2,1)} %get-tuple-element.31), channel_id=1, source_target_pairs={{0,2},{4,6},{1,3},{5,7},{14,12},{10,8},{15,13},{11,9},{16,18},{20,... | collective-permute-start | bytes 3145736 | tf_op jit(solution)/shard_map/ppermute | solution.py:85
  342.2 37.2 %collective-permute-start.12 = (bf16[2048,256]{0,1:T(8,128)(2,1)S(1)}, bf16[2048,256]{0,1:T(8,128)(2,1)S(1)}, u32[]{:S(2)}, u32[]{:S(2)}) collective-permute-start(bf16[2048,256]{0,1:T(8,128)(2,1)S(1)} %get-tuple-element.29), channel_id=1, source_target_pairs={{4,0},{5,1},{10,14},{11,15},{20,16},{21,17},{26,30},{27,31}} | collective-permute-start | bytes 3145736 | tf_op jit(solution)/shard_map/ppermute | solution.py:85
  367.6 24.9 %collective-permute-start.25 = (bf16[2048,256]{0,1:T(8,128)(2,1)S(1)}, bf16[2048,256]{0,1:T(8,128)(2,1)S(1)}, u32[]{:S(2)}, u32[]{:S(2)}) collective-permute-start(bf16[2048,256]{0,1:T(8,128)(2,1)S(1)} %get-tuple-element.30), channel_id=1, source_target_pairs={{4,0},{5,1},{10,14},{11,15},{20,16},{21,17},{26,30},{27,31}} | collective-permute-start | bytes 3145736 | tf_op jit(solution)/shard_map/ppermute | solution.py:85
  378.0 36.5 %collective-permute-start.34 = (bf16[2048,256]{0,1:T(8,128)(2,1)S(1)}, bf16[2048,256]{0,1:T(8,128)(2,1)S(1)}, u32[]{:S(2)}, u32[]{:S(2)}) collective-permute-start(bf16[2048,256]{0,1:T(8,128)(2,1)S(1)} %get-tuple-element.28), channel_id=1, source_target_pairs={{4,0},{5,1},{10,14},{11,15},{20,16},{21,17},{26,30},{27,31}} | collective-permute-start | bytes 3145736 | tf_op jit(solution)/shard_map/ppermute | solution.py:85
  427.3 30.9 %collective-permute-start.28 = (f32[2,256,256]{2,1,0:T(8,128)}, f32[2,256,256]{2,1,0:T(8,128)}, u32[]{:S(2)}, u32[]{:S(2)}) collective-permute-start(f32[2,256,256]{2,1,0:T(8,128)} %fusion.75), channel_id=1, source_target_pairs={{0,12},{1,13},{2,14},{3,15},{4,8},{5,9},{6,10},{7,11},{8,4},{9,5},... | collective-permute-start | bytes 1572872 | tf_op jit(solution)/shard_map/ppermute | solution.py:85
  429.0 28.0 %collective-permute-start.38 = (f32[256,256]{1,0:T(8,128)S(1)}, f32[256,256]{1,0:T(8,128)}, u32[]{:S(2)}, u32[]{:S(2)}) collective-permute-start(f32[256,256]{1,0:T(8,128)S(1)} %fusion.79), channel_id=1, source_target_pairs={{0,4},{1,5},{2,6},{3,7},{4,0},{5,1},{6,2},{7,3},{8,12},{9,13},{10,... | collective-permute-start | bytes 786440 | tf_op jit(solution)/shard_map/ppermute | solution.py:85
  (22 other events, 304.4 us)

commit v3 on v0

--- a/solution.py
+++ b/solution.py
@@ -1,10 +1,36 @@
+import functools
+
 import jax
 import jax.numpy as jnp
 from jax import lax
 from jax.sharding import PartitionSpec as P
 
 
-def per_device(sigma_root, lower1, mask1, inv1, lower2, mask2, link2, inv2, parent):
+def sum_rows(value, size):
+    if size != 4:
+        return lax.psum(value, "row")
+    for flip in (1, 3):
+        value = value + lax.ppermute(value, "row", [(r, r ^ flip) for r in range(size)])
+    return value
+
+
+def gather_rows(panel, size):
+    me = lax.axis_index("row")
+    up, down, ups, downs = panel, panel, [], []
+    for hop in range(1, size):
+        up = lax.ppermute(up, "row", [(r, r + 1) for r in range(hop - 1, size - 1)])
+        down = lax.ppermute(down, "row", [(r, r - 1) for r in range(1, size - hop + 1)])
+        ups.append(up)
+        downs.append(down)
+    whole = jnp.zeros((size,) + panel.shape, panel.dtype)
+    whole = lax.dynamic_update_index_in_dim(whole, panel, me, 0)
+    for hop in range(1, size):
+        block = jnp.where(me >= hop, ups[hop - 1], downs[size - hop - 1])
+        whole = lax.dynamic_update_index_in_dim(whole, block, lax.rem(me - hop + size, size), 0)
+    return whole.reshape(size * panel.shape[0], panel.shape[1])
+
+
+def per_device(size, sigma_root, lower1, mask1, inv1, lower2, mask2, link2, inv2, parent):
     block = inv1.shape[1]
     rows = sigma_root.shape[0]
     row_blocks = rows // block
@@ -28,15 +54,10 @@
     panel2 = make_panel(lower2, mask2, inv2)
     root_rows = lax.all_gather(sigma_root, "col", axis=1, tiled=True)
 
-    def root_product(panel):
-        return jnp.dot(
-            root_rows,
-            lax.all_gather(panel, "row", axis=0, tiled=True),
-            preferred_element_type=jnp.float32,
-        )
-
-    x_one = root_product(panel1)
-    x_two = root_product(panel2)
+    width = count1 * block
+    everything = gather_rows(jnp.concatenate([panel1, panel2], axis=1), size)
+    x_one = jnp.dot(root_rows, everything[:, :width], preferred_element_type=jnp.float32)
+    x_two = jnp.dot(root_rows, everything[:, width:], preferred_element_type=jnp.float32)
     off1 = (-x_one).astype(jnp.bfloat16)
     off1_blocks = off1.reshape(rows, count1, block)
     term1 = jnp.einsum(
@@ -45,7 +66,7 @@
         off1_blocks,
         preferred_element_type=jnp.float32,
     )
-    term1 = lax.psum(term1, "row")
+    term1 = sum_rows(term1, size)
     base1 = jnp.einsum("pcb,pcd->pbd", inv1, inv1, preferred_element_type=jnp.float32)
     diag1 = (base1 - term1).astype(jnp.bfloat16)
     link_u = jnp.einsum("kbc,kcd->kbd", link2, inv2, preferred_element_type=jnp.float32).astype(
@@ -72,7 +93,7 @@
         off2.reshape(rows, count2, block),
         preferred_element_type=jnp.float32,
     )
-    cross, pair = lax.psum((cross, pair), "row")
+    cross, pair = sum_rows(cross, size), sum_rows(pair, size)
     y_par = cross + jnp.einsum("kbc,kcd->kbd", par_diag, link_u, preferred_element_type=jnp.float32)
     par2 = (-y_par).astype(jnp.bfloat16)
     base2 = jnp.einsum("kcb,kcd->kbd", inv2, inv2, preferred_element_type=jnp.float32)
@@ -94,7 +115,7 @@
         P(),
     )
     return jax.shard_map(
-        per_device,
+        functools.partial(per_device, mesh.shape["row"]),
         mesh=mesh,
         in_specs=placed,
         out_specs=(

time: 532 us -> 359 us (0.67)
  waiting for transfers between devices: 441 us -> 212 us
  starting transfers between devices: 0.16 us -> 27.9 us
  other arithmetic: 1.56 us -> 20 us
  local copies, waits for them, and re-layouts: 12.1 us -> 22 us
    ppermute x0 -> x12, waiting for transfers between devices: none -> 212 us  [the longest x3 180 us: gather_rows(): lax.ppermute(down, 'row', [(r, r - 1) for r in range(1, size - hop + 1)])]
    all_gather x1, waiting for transfers between devices: 204 us -> 0.01 us  [per_device(): root_rows = lax.all_gather(sigma_root, 'col', axis=1, tiled=True)]
    all_gather x2 -> x0, waiting for transfers between devices: 188 us -> none  [root_product(): lax.all_gather(panel, 'row', axis=0, tiled=True)]
    psum x1 -> x0, waiting for transfers between devices: 48.7 us -> none  [per_device(): term1 = lax.psum(term1, 'row')]
    ppermute x0 -> x12, starting transfers between devices: none -> 27.8 us  [the longest x3 12.6 us: gather_rows(): up = lax.ppermute(up, 'row', [(r, r + 1) for r in range(hop - 1, size - 1)])]
    dynamic_update_slice x0 -> x4, other arithmetic: none -> 11.3 us  [the longest x3 9.49 us: gather_rows(): lax.dynamic_update_index_in_dim(whole, block, lax.rem(me - hop + size, si...]
  transfers between devices with their start and end apart: 4 -> 13, of which waited for: 4 -> 7; matrix products, arithmetic and copies ran while one was open for 8% -> 19% of each run, Pallas kernels for 0% -> 0%
where the time goes in v3:
time: 359 us; the launch traced here: 358 us
  waiting for transfers between devices  212 us (59%)
  matrix products  60.7 us (17%)
  starting transfers between devices  27.9 us (8%)
  local copies, waits for them, and re-layouts  22 us (6%)
  other arithmetic  20 us (6%)
  between operations  14.9 us (4%)
    ppermute x3, waiting for transfers between devices, gather_rows(): lax.ppermute(down, 'row', [(r, r - 1) for r in range(1, size - hop + 1)])  180 us
    ppermute x6, waiting for transfers between devices, sum_rows(): lax.ppermute(value, 'row', [(r, r ^ flip) for r in range(size)])  31.3 us
    dot_general x1, matrix products, per_device(): jnp.dot(root_rows, everything[:, :width], preferred_element_type=jnp.floa...  24.1 us
    dot_general x1, matrix products, per_device(): jnp.dot(root_rows, everything[:, width:], preferred_element_type=jnp.floa...  17.5 us
    ppermute x3, starting transfers between devices, gather_rows(): up = lax.ppermute(up, 'row', [(r, r + 1) for r in range(hop - 1, size - 1)])  12.6 us
    dynamic_update_slice x3, other arithmetic, gather_rows(): lax.dynamic_update_index_in_dim(whole, block, lax.rem(me - hop + size, si...  9.49 us
    ppermute x3, starting transfers between devices, gather_rows(): lax.ppermute(down, 'row', [(r, r - 1) for r in range(1, size - hop + 1)])  8.72 us
    unnamed x38, local copies, waits for them, and re-layouts  8.02 us
  transfers between devices with their start and end apart: 13, of which 7 were waited for; matrix products, arithmetic and copies ran while one was open for 19% of the time, Pallas kernels for 0%

profile of v3, /device:TPU:10, one launch (start us, length us, event | category | flops | bytes accessed | tf_op | source)
XLA Modules:
  0.0 357.7 jit_solution(16173328759233279117)
XLA Ops:
  8.9 2.3 convolution_convert_fusion
  11.1 2.9 copy.22
  14.9 1.9 convolution_convert_fusion.1
  19.8 2.4 collective-permute-start.1
  22.1 3.5 collective-permute-start
  25.6 65.9 %collective-permute-done.1 = bf16[2048,768]{1,0:T(8,128)(2,1)S(1)} collective-permute-done((bf16[2048,768]{1,0:T(8,128)(2,1)S(1)}, bf16[2048,768]{1,0:T(8,128)(2,1)S(1)}, u32[]{:S(2)}, u32[]{:S(2)}) %collective-permute-start.1) | collective-permute-done | bytes 3145760 | tf_op jit(solution)/shard_map/ppermute | solution.py:22
  93.1 2.3 collective-permute-start.2
  95.5 6.8 %collective-permute-start.4 = (bf16[2048,768]{1,0:T(8,128)(2,1)S(1)}, bf16[2048,768]{1,0:T(8,128)(2,1)}, u32[]{:S(2)}, u32[]{:S(2)}) collective-permute-start(bf16[2048,768]{1,0:T(8,128)(2,1)S(1)} %collective-permute-done), channel_id=1, source_target_pairs={{4,8},{8,12},{5,9},{9,13},{6,10},{10,14},{7,11},{11,15},{20,24},{2... | collective-permute-start | bytes 9437192 | tf_op jit(solution)/shard_map/ppermute | solution.py:21
  102.3 61.9 %collective-permute-done.2 = bf16[2048,768]{1,0:T(8,128)(2,1)} collective-permute-done((bf16[2048,768]{1,0:T(8,128)(2,1)S(1)}, bf16[2048,768]{1,0:T(8,128)(2,1)}, u32[]{:S(2)}, u32[]{:S(2)}) %collective-permute-start.2) | collective-permute-done | bytes 3145760 | tf_op jit(solution)/shard_map/ppermute | solution.py:22
  164.2 4.0 %collective-permute-start.3 = (bf16[2048,768]{1,0:T(8,128)(2,1)}, bf16[2048,768]{1,0:T(8,128)(2,1)}, u32[]{:S(2)}, u32[]{:S(2)}) collective-permute-start(bf16[2048,768]{1,0:T(8,128)(2,1)} %collective-permute-done.2), channel_id=1, source_target_pairs={{4,0},{5,1},{6,2},{7,3},{20,16},{21,17},{22,18},{23,19}} | collective-permute-start | bytes 9437192 | tf_op jit(solution)/shard_map/ppermute | solution.py:22
  168.2 2.3 collective-permute-start.5
  172.9 5.3 %broadcast_in_dim.20 = bf16[4,2048,768]{2,1,0:T(8,128)(2,1)} broadcast(bf16[]{:T(256)} %constant.35.clone.1), dimensions={} | broadcast | bytes 12582914 | tf_op jit(solution)/shard_map/broadcast_in_dim | solution.py:25
  178.1 1.9 bitcast_dynamic-update-slice_fusion.3
  180.0 52.5 %collective-permute-done.3 = bf16[2048,768]{1,0:T(8,128)(2,1)} collective-permute-done((bf16[2048,768]{1,0:T(8,128)(2,1)}, bf16[2048,768]{1,0:T(8,128)(2,1)}, u32[]{:S(2)}, u32[]{:S(2)}) %collective-permute-start.3) | collective-permute-done | bytes 3145760 | tf_op jit(solution)/shard_map/ppermute | solution.py:22
  232.5 2.6 bitcast_dynamic-update-slice_fusion.2
  235.1 4.4 %bitcast_dynamic-update-slice_fusion.1 = bf16[4,2048,768]{2,1,0:T(8,128)(2,1)} fusion(bf16[4,2048,768]{2,1,0:T(8,128)(2,1)} %bitcast_dynamic-update-slice_fusion.2, s32[]{:T(128)S(6)} %select_n.53, bf16[2048,768]{1,0:T(8,128)(2,1)} %collective-permute-done.4, bf16[2048,768]{1,0:T(8,128)(2,1)} %collective-permute-done.2, pred[]{:T(512)S(6)} %ge.10), kind=kLoop, calls=%fused_computation.7 | loop fusion | flops 1572864 | bytes 9437189 | tf_op jit(solution)/shard_map/jit(dynamic_update_index_in_dim)/dynamic_update_slice | solution.py:29
  239.4 2.5 bitcast_dynamic-update-slice_fusion
  242.0 24.1 %negate_convert_fusion = bf16[512,2048]{1,0:T(8,128)(2,1)S(1)} fusion(bf16[2048,8192]{1,0:T(8,128)(2,1)} %all-gather.2.cloned.1.call-done, bf16[8192,768]{1,0:T(8,128)(2,1)} %bitcast.105), kind=kOutput, calls=%fused_computation.4 | convolution fusion | flops 17181966336 | bytes 44040192 | tf_op jit(solution)/shard_map/dot_general | solution.py:59
  266.0 3.9 %copy.31 = bf16[2048,2,256]{2,1,0:T(2,128)(2,1)} copy(bf16[2048,2,256]{0,2,1:T(8,128)(2,1)S(1)} %bitcast.102) | data formatting | bytes 4194304 | tf_op jit(solution)/shard_map/reshape | solution.py:62
  269.9 3.3 fusion.19
  273.2 4.4 %collective-permute-start.6 = (f32[2,256,256]{2,1,0:T(8,128)}, f32[2,256,256]{2,1,0:T(8,128)}, u32[]{:S(2)}, u32[]{:S(2)}) collective-permute-start(f32[2,256,256]{2,1,0:T(8,128)} %fusion.19), channel_id=1, source_target_pairs={{0,4},{4,0},{8,12},{12,8},{1,5},{5,1},{9,13},{13,9},{2,6},{6,2},{1... | collective-permute-start | bytes 1572872 | tf_op jit(solution)/shard_map/ppermute | solution.py:13
  277.6 2.3 fusion.33
  283.1 17.5 %fusion.15 = bf16[2048,256]{0,1:T(8,128)(2,1)} fusion(f32[2048,256]{0,1:T(8,128)} %convolution_bitcast_fusion, bf16[2048,8192]{1,0:T(8,128)(2,1)} %all-gather.2.cloned.1.call-done, bf16[8192,768]{1,0:T(8,128)(2,1)} %bitcast.106), kind=kOutput, calls=%fused_computation.15 | convolution fusion | flops 8591507456 | bytes 40894464 | tf_op jit(solution)/shard_map/dot_general | solution.py:60
  300.6 2.6 convolution_bitcast_fusion.4
  303.1 2.1 add.76
  306.5 2.0 collective-permute-start.8
  309.7 2.3 copy.27
  312.0 2.5 copy.26
  314.5 4.0 %collective-permute-done.10 = f32[1,256,256]{2,1,0:T(8,128)} collective-permute-done((f32[1,256,256]{2,1,0:T(8,128)}, f32[1,256,256]{2,1,0:T(8,128)}, u32[]{:S(2)}, u32[]{:S(2)}) %collective-permute-start.10) | collective-permute-done | bytes 262176 | tf_op jit(solution)/shard_map/ppermute | solution.py:13
  319.6 10.2 %collective-permute-done.8 = f32[1,256,256]{2,1,0:T(8,128)S(1)} collective-permute-done((f32[1,256,256]{2,1,0:T(8,128)}, f32[1,256,256]{2,1,0:T(8,128)S(1)}, u32[]{:S(2)}, u32[]{:S(2)}) %collective-permute-start.8) | collective-permute-done | bytes 262176 | tf_op jit(solution)/shard_map/ppermute | solution.py:13
  330.9 10.4 %collective-permute-done.7 = f32[2,256,256]{2,1,0:T(8,128)} collective-permute-done((f32[2,256,256]{2,1,0:T(8,128)}, f32[2,256,256]{2,1,0:T(8,128)}, u32[]{:S(2)}, u32[]{:S(2)}) %collective-permute-start.7) | collective-permute-done | bytes 524320 | tf_op jit(solution)/shard_map/ppermute | solution.py:13
  343.3 6.7 %collective-permute-done.9 = f32[1,256,256]{2,1,0:T(8,128)S(1)} collective-permute-done((f32[1,256,256]{2,1,0:T(8,128)S(1)}, f32[1,256,256]{2,1,0:T(8,128)S(1)}, u32[]{:S(2)}, u32[]{:S(2)}) %collective-permute-start.9) | collective-permute-done | bytes 262176 | tf_op jit(solution)/shard_map/ppermute | solution.py:13
  (65 shorter events, 19.5 us)
Async XLA Ops:
  7.2 1.6 copy-start
  7.2 1.7 copy-start.14
  7.2 234.8 %all-gather.2.cloned.1.call-start = ((), (), s32[]{:S(2)}) async-start(), calls=%async_computation | async-start | bytes 41943040 | tf_op jit(solution)/shard_map/all_gather | solution.py:55
  11.1 3.8 %copy-start.7 = (bf16[1,256,256]{2,1,0:T(8,128)(2,1)S(1)}, bf16[1,256,256]{2,1,0:T(8,128)(2,1)}, u32[]{:S(2)}) copy-start(bf16[1,256,256]{2,1,0:T(8,128)(2,1)} %param.16) | copy-start | bytes 393220
  18.1 152.4 %copy-start.15 = (s32[4]{0:T(128)S(1)}, s32[4]{0:T(128)}, u32[]{:S(2)}) copy-start(s32[4]{0:T(128)} %param.17) | copy-start | bytes 52
  19.8 71.7 %collective-permute-start.1 = (bf16[2048,768]{1,0:T(8,128)(2,1)S(1)}, bf16[2048,768]{1,0:T(8,128)(2,1)S(1)}, u32[]{:S(2)}, u32[]{:S(2)}) collective-permute-start(bf16[2048,768]{1,0:T(8,128)(2,1)S(1)} %pad_maximum_fusion), channel_id=1, source_target_pairs={{4,0},{8,4},{12,8},{5,1},{9,5},{13,9},{6,2},{10,6},{14,10},{7,3},{... | collective-permute-start | bytes 9437192 | tf_op jit(solution)/shard_map/ppermute | solution.py:22
  22.1 73.3 %collective-permute-start = (bf16[2048,768]{1,0:T(8,128)(2,1)S(1)}, bf16[2048,768]{1,0:T(8,128)(2,1)S(1)}, u32[]{:S(2)}, u32[]{:S(2)}) collective-permute-start(bf16[2048,768]{1,0:T(8,128)(2,1)S(1)} %pad_maximum_fusion), channel_id=1, source_target_pairs={{0,4},{4,8},{8,12},{1,5},{5,9},{9,13},{2,6},{6,10},{10,14},{3,7},{... | collective-permute-start | bytes 9437192 | tf_op jit(solution)/shard_map/ppermute | solution.py:21
  91.5 1.6 copy-start.2
  93.1 71.1 %collective-permute-start.2 = (bf16[2048,768]{1,0:T(8,128)(2,1)S(1)}, bf16[2048,768]{1,0:T(8,128)(2,1)}, u32[]{:S(2)}, u32[]{:S(2)}) collective-permute-start(bf16[2048,768]{1,0:T(8,128)(2,1)S(1)} %collective-permute-done.1), channel_id=1, source_target_pairs={{4,0},{8,4},{5,1},{9,5},{6,2},{10,6},{7,3},{11,7},{20,16},{24,20},... | collective-permute-start | bytes 9437192 | tf_op jit(solution)/shard_map/ppermute | solution.py:22
  95.5 68.7 %copy-start.4 = (bf16[2048,768]{1,0:T(8,128)(2,1)}, bf16[2048,768]{1,0:T(8,128)(2,1)S(1)}, u32[]{:S(2)}) copy-start(bf16[2048,768]{1,0:T(8,128)(2,1)S(1)} %collective-permute-done) | copy-start | bytes 9437188
  95.5 72.7 %collective-permute-start.4 = (bf16[2048,768]{1,0:T(8,128)(2,1)S(1)}, bf16[2048,768]{1,0:T(8,128)(2,1)}, u32[]{:S(2)}, u32[]{:S(2)}) collective-permute-start(bf16[2048,768]{1,0:T(8,128)(2,1)S(1)} %collective-permute-done), channel_id=1, source_target_pairs={{4,8},{8,12},{5,9},{9,13},{6,10},{10,14},{7,11},{11,15},{20,24},{2... | collective-permute-start | bytes 9437192 | tf_op jit(solution)/shard_map/ppermute | solution.py:21
  164.2 68.3 %collective-permute-start.3 = (bf16[2048,768]{1,0:T(8,128)(2,1)}, bf16[2048,768]{1,0:T(8,128)(2,1)}, u32[]{:S(2)}, u32[]{:S(2)}) collective-permute-start(bf16[2048,768]{1,0:T(8,128)(2,1)} %collective-permute-done.2), channel_id=1, source_target_pairs={{4,0},{5,1},{6,2},{7,3},{20,16},{21,17},{22,18},{23,19}} | collective-permute-start | bytes 9437192 | tf_op jit(solution)/shard_map/ppermute | solution.py:22
  168.2 71.2 %collective-permute-start.5 = (bf16[2048,768]{1,0:T(8,128)(2,1)}, bf16[2048,768]{1,0:T(8,128)(2,1)}, u32[]{:S(2)}, u32[]{:S(2)}) collective-permute-start(bf16[2048,768]{1,0:T(8,128)(2,1)} %collective-permute-done.4), channel_id=1, source_target_pairs={{8,12},{9,13},{10,14},{11,15},{24,28},{25,29},{26,30},{27,31}} | collective-permute-start | bytes 9437192 | tf_op jit(solution)/shard_map/ppermute | solution.py:21
  172.9 5.3 %copy-start.1 = (bf16[2048,256]{1,0:T(8,128)(2,1)S(1)}, bf16[2048,256]{1,0:T(8,128)(2,1)}, u32[]{:S(2)}) copy-start(bf16[2048,256]{1,0:T(8,128)(2,1)} %copy.23) | copy-start | bytes 3145732
  178.1 54.3 %copy-start.5 = (bf16[2048,768]{1,0:T(8,128)(2,1)S(1)}, bf16[2048,768]{1,0:T(8,128)(2,1)}, u32[]{:S(2)}) copy-start(bf16[2048,768]{1,0:T(8,128)(2,1)} %copy-done.4) | copy-start | bytes 9437188
  235.1 4.4 %copy-start.3 = (bf16[2048,768]{1,0:T(8,128)(2,1)S(1)}, bf16[2048,768]{1,0:T(8,128)(2,1)}, u32[]{:S(2)}) copy-start(bf16[2048,768]{1,0:T(8,128)(2,1)} %copy-done.2) | copy-start | bytes 9437188
  269.9 7.6 %copy-start.6 = (bf16[2048,2,256]{2,1,0:T(2,128)(2,1)S(1)}, bf16[2048,2,256]{2,1,0:T(2,128)(2,1)}, u32[]{:S(2)}) copy-start(bf16[2048,2,256]{2,1,0:T(2,128)(2,1)} %copy.31) | copy-start | bytes 6291460
  273.2 29.9 %collective-permute-start.6 = (f32[2,256,256]{2,1,0:T(8,128)}, f32[2,256,256]{2,1,0:T(8,128)}, u32[]{:S(2)}, u32[]{:S(2)}) collective-permute-start(f32[2,256,256]{2,1,0:T(8,128)} %fusion.19), channel_id=1, source_target_pairs={{0,4},{4,0},{8,12},{12,8},{1,5},{5,1},{9,13},{13,9},{2,6},{6,2},{1... | collective-permute-start | bytes 1572872 | tf_op jit(solution)/shard_map/ppermute | solution.py:13
  279.9 1.4 copy-start.10
  300.6 4.7 %copy-start.11 = (bf16[1,2048,256]{2,0,1:T(2,128)(2,1)S(1)}, bf16[1,2048,256]{2,0,1:T(2,128)(2,1)}, u32[]{:S(2)}) copy-start(bf16[1,2048,256]{2,0,1:T(2,128)(2,1)} %copy-done.10) | copy-start | bytes 3145732
  300.6 7.9 %copy-start.8 = (bf16[1,256,256]{2,1,0:T(8,128)(2,1)S(1)}, bf16[1,256,256]{2,1,0:T(8,128)(2,1)}, u32[]{:S(2)}) copy-start(bf16[1,256,256]{2,1,0:T(8,128)(2,1)} %param.16) | copy-start | bytes 393220
  303.1 15.4 %collective-permute-start.10 = (f32[1,256,256]{2,1,0:T(8,128)}, f32[1,256,256]{2,1,0:T(8,128)}, u32[]{:S(2)}, u32[]{:S(2)}) collective-permute-start(f32[1,256,256]{2,1,0:T(8,128)} %convolution_bitcast_fusion.4), channel_id=1, source_target_pairs={{0,4},{4,0},{8,12},{12,8},{1,5},{5,1},{9,13},{13,9},{2,6},{6,2},{1... | collective-permute-start | bytes 786440 | tf_op jit(solution)/shard_map/ppermute | solution.py:13
  305.2 36.1 %collective-permute-start.7 = (f32[2,256,256]{2,1,0:T(8,128)}, f32[2,256,256]{2,1,0:T(8,128)}, u32[]{:S(2)}, u32[]{:S(2)}) collective-permute-start(f32[2,256,256]{2,1,0:T(8,128)} %add.76), channel_id=1, source_target_pairs={{0,12},{4,8},{8,4},{12,0},{1,13},{5,9},{9,5},{13,1},{2,14},{6,10},... | collective-permute-start | bytes 1572872 | tf_op jit(solution)/shard_map/ppermute | solution.py:13
  306.5 23.4 %collective-permute-start.8 = (f32[1,256,256]{2,1,0:T(8,128)}, f32[1,256,256]{2,1,0:T(8,128)S(1)}, u32[]{:S(2)}, u32[]{:S(2)}) collective-permute-start(f32[1,256,256]{2,1,0:T(8,128)} %convolution_bitcast_fusion.5), channel_id=1, source_target_pairs={{0,4},{4,0},{8,12},{12,8},{1,5},{5,1},{9,13},{13,9},{2,6},{6,2},{1... | collective-permute-start | bytes 786440 | tf_op jit(solution)/shard_map/ppermute | solution.py:13
  314.5 35.5 %copy-start.9 = (f32[1,256,256]{2,1,0:T(8,128)S(1)}, f32[1,256,256]{2,1,0:T(8,128)}, u32[]{:S(2)}) copy-start(f32[1,256,256]{2,1,0:T(8,128)} %convolution_bitcast_fusion.2) | copy-start | bytes 786436
  319.6 30.4 %collective-permute-start.11 = (f32[1,256,256]{2,1,0:T(8,128)S(1)}, f32[1,256,256]{2,1,0:T(8,128)S(1)}, u32[]{:S(2)}, u32[]{:S(2)}) collective-permute-start(f32[1,256,256]{2,1,0:T(8,128)S(1)} %add.82), channel_id=1, source_target_pairs={{0,12},{4,8},{8,4},{12,0},{1,13},{5,9},{9,5},{13,1},{2,14},{6,10},... | collective-permute-start | bytes 786440 | tf_op jit(solution)/shard_map/ppermute | solution.py:13
  330.8 19.1 %collective-permute-start.9 = (f32[1,256,256]{2,1,0:T(8,128)S(1)}, f32[1,256,256]{2,1,0:T(8,128)S(1)}, u32[]{:S(2)}, u32[]{:S(2)}) collective-permute-start(f32[1,256,256]{2,1,0:T(8,128)S(1)} %add.79), channel_id=1, source_target_pairs={{0,12},{4,8},{8,4},{12,0},{1,13},{5,9},{9,5},{13,1},{2,14},{6,10},... | collective-permute-start | bytes 786440 | tf_op jit(solution)/shard_map/ppermute | solution.py:13
  342.6 8.3 %copy-start.13 = (bf16[2,256,256]{2,1,0:T(8,128)(2,1)}, bf16[2,256,256]{2,1,0:T(8,128)(2,1)S(1)}, u32[]{:S(2)}) copy-start(bf16[2,256,256]{2,1,0:T(8,128)(2,1)S(1)} %subtract_convert_fusion) | copy-start | bytes 786436
  350.0 0.9 copy-start.12
Sparse Core Ops, SparseCore 0:
  9.6 202.6 all-gather.1

commit v4 on v3

--- a/solution.py
+++ b/solution.py
@@ -6,22 +6,28 @@
 from jax.sharding import PartitionSpec as P
 
 
+def exchange(value, flip):
+    return value + lax.ppermute(value, "row", [(r, r ^ flip) for r in range(4)])
+
+
 def sum_rows(value, size):
     if size != 4:
         return lax.psum(value, "row")
-    for flip in (1, 3):
-        value = value + lax.ppermute(value, "row", [(r, r ^ flip) for r in range(size)])
-    return value
+    return exchange(exchange(value, 1), 3)
 
 
-def gather_rows(panel, size):
-    me = lax.axis_index("row")
+def hop_rows(panel, size):
     up, down, ups, downs = panel, panel, [], []
     for hop in range(1, size):
         up = lax.ppermute(up, "row", [(r, r + 1) for r in range(hop - 1, size - 1)])
         down = lax.ppermute(down, "row", [(r, r - 1) for r in range(1, size - hop + 1)])
         ups.append(up)
         downs.append(down)
+    return ups, downs
+
+
+def collect_rows(panel, ups, downs, size):
+    me = lax.axis_index("row")
     whole = jnp.zeros((size,) + panel.shape, panel.dtype)
     whole = lax.dynamic_update_index_in_dim(whole, panel, me, 0)
     for hop in range(1, size):
@@ -54,10 +60,11 @@
     panel2 = make_panel(lower2, mask2, inv2)
     root_rows = lax.all_gather(sigma_root, "col", axis=1, tiled=True)
 
-    width = count1 * block
-    everything = gather_rows(jnp.concatenate([panel1, panel2], axis=1), size)
-    x_one = jnp.dot(root_rows, everything[:, :width], preferred_element_type=jnp.float32)
-    x_two = jnp.dot(root_rows, everything[:, width:], preferred_element_type=jnp.float32)
+    ups, downs = hop_rows(panel1, size)
+    next_panel, ups[-1], downs[-1] = lax.optimization_barrier((panel2, ups[-1], downs[-1]))
+    every1 = collect_rows(panel1, ups, downs, size)
+    every2 = collect_rows(next_panel, *hop_rows(next_panel, size), size)
+    x_one = jnp.dot(root_rows, every1, preferred_element_type=jnp.float32)
     off1 = (-x_one).astype(jnp.bfloat16)
     off1_blocks = off1.reshape(rows, count1, block)
     term1 = jnp.einsum(
@@ -66,12 +73,6 @@
         off1_blocks,
         preferred_element_type=jnp.float32,
     )
-    term1 = sum_rows(term1, size)
-    base1 = jnp.einsum("pcb,pcd->pbd", inv1, inv1, preferred_element_type=jnp.float32)
-    diag1 = (base1 - term1).astype(jnp.bfloat16)
-    link_u = jnp.einsum("kbc,kcd->kbd", link2, inv2, preferred_element_type=jnp.float32).astype(
-        jnp.bfloat16
-    )
     local_parent = lax.dynamic_slice_in_dim(parent, col_id * count2, count2) - col_id * count1
     pick = (local_parent[:, None] == jnp.arange(count1, dtype=jnp.int32)[None, :]).astype(
         jnp.bfloat16
@@ -79,21 +80,36 @@
     par_off = jnp.einsum(
         "kp,rpb->rkb", pick, off1_blocks, preferred_element_type=jnp.float32
     ).astype(jnp.bfloat16)
+    panel2_blocks = panel2.reshape(rows, count2, block)
+    cross = jnp.einsum("rkb,rkd->kbd", par_off, panel2_blocks, preferred_element_type=jnp.float32)
+    half = rows // 2
+    terms = jnp.concatenate([term1, cross], axis=0)
+    if size == 4:
+        terms = exchange(terms, 1)
+    top = jnp.dot(root_rows[:half], every2, preferred_element_type=jnp.float32)
+    top, terms = lax.optimization_barrier((top, terms))
+    terms = exchange(terms, 3) if size == 4 else lax.psum(terms, "row")
+    bottom = jnp.dot(root_rows[half:], every2, preferred_element_type=jnp.float32)
+    x_two = jnp.concatenate([top, bottom], axis=0)
+    term1, cross = terms[:count1], terms[count1:]
+    base1 = jnp.einsum("pcb,pcd->pbd", inv1, inv1, preferred_element_type=jnp.float32)
+    diag1 = (base1 - term1).astype(jnp.bfloat16)
+    link_u = jnp.einsum("kbc,kcd->kbd", link2, inv2, preferred_element_type=jnp.float32).astype(
+        jnp.bfloat16
+    )
     par_diag = jnp.einsum("kp,pbd->kbd", pick, diag1, preferred_element_type=jnp.float32).astype(
         jnp.bfloat16
     )
-    panel2_blocks = panel2.reshape(rows, count2, block)
     extra = jnp.einsum("rkb,kbd->rkd", par_off, link_u, preferred_element_type=jnp.float32)
     y_root = x_two + extra.reshape(rows, count2 * block)
     off2 = (-y_root).astype(jnp.bfloat16)
-    cross = jnp.einsum("rkb,rkd->kbd", par_off, panel2_blocks, preferred_element_type=jnp.float32)
     pair = jnp.einsum(
         "rkb,rkd->kbd",
         panel2_blocks,
         off2.reshape(rows, count2, block),
         preferred_element_type=jnp.float32,
     )
-    cross, pair = sum_rows(cross, size), sum_rows(pair, size)
+    pair = sum_rows(pair, size)
     y_par = cross + jnp.einsum("kbc,kcd->kbd", par_diag, link_u, preferred_element_type=jnp.float32)
     par2 = (-y_par).astype(jnp.bfloat16)
     base2 = jnp.einsum("kcb,kcd->kbd", inv2, inv2, preferred_element_type=jnp.float32)

time: 359 us -> 361 us (level)
  waiting for transfers between devices: 212 us -> 182 us
  starting transfers between devices: 27.9 us -> 49.9 us
  matrix products: 60.7 us -> 65.8 us
  local copies, waits for them, and re-layouts: 22 us -> 26.7 us
    ppermute x12 -> x16, waiting for transfers between devices: 212 us -> 182 us  [the longest x6 88.8 us: hop_rows(): up = lax.ppermute(up, 'row', [(r, r + 1) for r in range(hop - 1, size - 1)])]
    ppermute x12 -> x16, starting transfers between devices: 27.8 us -> 49.9 us  [the longest x6 21 us: hop_rows(): lax.ppermute(down, 'row', [(r, r - 1) for r in range(1, size - hop + 1)])]
    dot_general x2 -> x3, matrix products: 41.6 us -> 47.3 us  [the longest x1 24.8 us: per_device(): x_one = jnp.dot(root_rows, every1, preferred_element_type=jnp.float32)]
    broadcast_in_dim x1 -> x3, local copies, waits for them, and re-layouts: 5.27 us -> 8.67 us  [the longest x2 6.16 us: collect_rows(): whole = jnp.zeros((size,) + panel.shape, panel.dtype)]
    unnamed x38 -> x46, local copies, waits for them, and re-layouts: 8.02 us -> 6.3 us
    dynamic_update_slice x4 -> x6, other arithmetic: 11.3 us -> 12.5 us  [collect_rows(): lax.dynamic_update_index_in_dim(whole, block, lax.rem(me - hop + size, si...]
  transfers between devices with their start and end apart: 13 -> 17, of which waited for: 7 -> 12; matrix products, arithmetic and copies ran while one was open for 19% -> 20% of each run, Pallas kernels for 0% -> 0%
where the time goes in v4:
time: 361 us; the launch traced here: 360 us
  waiting for transfers between devices  182 us (50%)
  matrix products  65.8 us (18%)
  starting transfers between devices  49.9 us (14%)
  local copies, waits for them, and re-layouts  26.7 us (7%)
  other arithmetic  20.5 us (6%)
  between operations  15 us (4%)
    ppermute x6, waiting for transfers between devices, hop_rows(): up = lax.ppermute(up, 'row', [(r, r + 1) for r in range(hop - 1, size - 1)])  88.8 us
    ppermute x6, waiting for transfers between devices, hop_rows(): lax.ppermute(down, 'row', [(r, r - 1) for r in range(1, size - hop + 1)])  68.6 us
    dot_general x1, matrix products, per_device(): x_one = jnp.dot(root_rows, every1, preferred_element_type=jnp.float32)  24.8 us
    ppermute x4, waiting for transfers between devices, exchange(): return value + lax.ppermute(value, 'row', [(r, r ^ flip) for r in range(4)])  24.2 us
    ppermute x6, starting transfers between devices, hop_rows(): lax.ppermute(down, 'row', [(r, r - 1) for r in range(1, size - hop + 1)])  21 us
    ppermute x6, starting transfers between devices, hop_rows(): up = lax.ppermute(up, 'row', [(r, r + 1) for r in range(hop - 1, size - 1)])  15.4 us
    ppermute x4, starting transfers between devices, exchange(): return value + lax.ppermute(value, 'row', [(r, r ^ flip) for r in range(4)])  13.5 us
    dot_general x1, matrix products, per_device(): jnp.dot(root_rows[half:], every2, preferred_element_type=jnp.float32)  12.9 us
  transfers between devices with their start and end apart: 17, of which 12 were waited for; matrix products, arithmetic and copies ran while one was open for 20% of the time, Pallas kernels for 0%

profile of v4, /device:TPU:10, one launch (start us, length us, event | category | flops | bytes accessed | tf_op | source)
XLA Modules:
  0.0 360.4 jit_solution(6678694728456640266)
XLA Ops:
  8.8 2.6 convolution_convert_fusion
  11.4 2.5 copy.23
  13.9 3.5 collective-permute-start
  17.4 2.5 collective-permute-start.3
  19.8 43.5 %collective-permute-done = bf16[2048,512]{1,0:T(8,128)(2,1)S(1)} collective-permute-done((bf16[2048,512]{1,0:T(8,128)(2,1)}, bf16[2048,512]{1,0:T(8,128)(2,1)S(1)}, u32[]{:S(2)}, u32[]{:S(2)}) %collective-permute-start) | collective-permute-done | bytes 2097184 | tf_op jit(solution)/shard_map/ppermute | solution.py:22
  63.3 4.8 %collective-permute-start.1 = (bf16[2048,512]{1,0:T(8,128)(2,1)S(1)}, bf16[2048,512]{1,0:T(8,128)(2,1)}, u32[]{:S(2)}, u32[]{:S(2)}) collective-permute-start(bf16[2048,512]{1,0:T(8,128)(2,1)S(1)} %collective-permute-done), channel_id=1, source_target_pairs={{4,8},{8,12},{5,9},{9,13},{6,10},{10,14},{7,11},{11,15},{20,24},{2... | collective-permute-start | bytes 6291464 | tf_op jit(solution)/shard_map/ppermute | solution.py:22
  71.5 39.5 %collective-permute-done.1 = bf16[2048,512]{1,0:T(8,128)(2,1)} collective-permute-done((bf16[2048,512]{1,0:T(8,128)(2,1)S(1)}, bf16[2048,512]{1,0:T(8,128)(2,1)}, u32[]{:S(2)}, u32[]{:S(2)}) %collective-permute-start.1) | collective-permute-done | bytes 2097184 | tf_op jit(solution)/shard_map/ppermute | solution.py:22
  112.9 4.9 %collective-permute-done.4 = bf16[2048,512]{1,0:T(8,128)(2,1)} collective-permute-done((bf16[2048,512]{1,0:T(8,128)(2,1)S(1)}, bf16[2048,512]{1,0:T(8,128)(2,1)}, u32[]{:S(2)}, u32[]{:S(2)}) %collective-permute-start.4) | collective-permute-done | bytes 2097184 | tf_op jit(solution)/shard_map/ppermute | solution.py:23
  117.9 3.5 collective-permute-start.5
  124.0 39.6 %collective-permute-done.5 = bf16[2048,512]{1,0:T(8,128)(2,1)} collective-permute-done((bf16[2048,512]{1,0:T(8,128)(2,1)}, bf16[2048,512]{1,0:T(8,128)(2,1)}, u32[]{:S(2)}, u32[]{:S(2)}) %collective-permute-start.5) | collective-permute-done | bytes 2097184 | tf_op jit(solution)/shard_map/ppermute | solution.py:23
  163.5 4.4 %collective-permute-start.7 = (bf16[2048,256]{1,0:T(8,128)(2,1)S(1)}, bf16[2048,256]{1,0:T(8,128)(2,1)}, u32[]{:S(2)}, u32[]{:S(2)}) collective-permute-start(bf16[2048,256]{1,0:T(8,128)(2,1)S(1)} %convolution_convert_fusion.1), channel_id=1, source_target_pairs={{4,0},{8,4},{12,8},{5,1},{9,5},{13,9},{6,2},{10,6},{14,10},{7,3},{... | collective-permute-start | bytes 3145736 | tf_op jit(solution)/shard_map/ppermute | solution.py:23
  168.0 2.5 copy.22
  172.9 3.9 %broadcast_in_dim.36 = bf16[4,2048,512]{2,1,0:T(8,128)(2,1)} broadcast(bf16[]{:T(256)} %constant.46.clone.1), dimensions={} | broadcast | bytes 8388610 | tf_op jit(solution)/shard_map/broadcast_in_dim | solution.py:31
  180.2 7.6 %collective-permute-done.7 = bf16[2048,256]{1,0:T(8,128)(2,1)} collective-permute-done((bf16[2048,256]{1,0:T(8,128)(2,1)S(1)}, bf16[2048,256]{1,0:T(8,128)(2,1)}, u32[]{:S(2)}, u32[]{:S(2)}) %collective-permute-start.7) | collective-permute-done | bytes 1048608 | tf_op jit(solution)/shard_map/ppermute | solution.py:23
  187.8 4.4 %collective-permute-start.8 = (bf16[2048,256]{1,0:T(8,128)(2,1)}, bf16[2048,256]{1,0:T(8,128)(2,1)S(1)}, u32[]{:S(2)}, u32[]{:S(2)}) collective-permute-start(bf16[2048,256]{1,0:T(8,128)(2,1)} %collective-permute-done.7), channel_id=1, source_target_pairs={{4,0},{8,4},{5,1},{9,5},{6,2},{10,6},{7,3},{11,7},{20,16},{24,20},... | collective-permute-start | bytes 3145736 | tf_op jit(solution)/shard_map/ppermute | solution.py:23
  194.2 3.6 bitcast_dynamic-update-slice_fusion.1
  197.7 4.4 %collective-permute-done.6 = bf16[2048,256]{1,0:T(8,128)(2,1)S(1)} collective-permute-done((bf16[2048,256]{1,0:T(8,128)(2,1)S(1)}, bf16[2048,256]{1,0:T(8,128)(2,1)S(1)}, u32[]{:S(2)}, u32[]{:S(2)}) %collective-permute-start.6) | collective-permute-done | bytes 1048608 | tf_op jit(solution)/shard_map/ppermute | solution.py:22
  204.4 7.0 %collective-permute-done.8 = bf16[2048,256]{1,0:T(8,128)(2,1)S(1)} collective-permute-done((bf16[2048,256]{1,0:T(8,128)(2,1)}, bf16[2048,256]{1,0:T(8,128)(2,1)S(1)}, u32[]{:S(2)}, u32[]{:S(2)}) %collective-permute-start.8) | collective-permute-done | bytes 1048608 | tf_op jit(solution)/shard_map/ppermute | solution.py:23
  211.4 4.3 %collective-permute-start.9 = (bf16[2048,256]{1,0:T(8,128)(2,1)S(1)}, bf16[2048,256]{1,0:T(8,128)(2,1)S(1)}, u32[]{:S(2)}, u32[]{:S(2)}) collective-permute-start(bf16[2048,256]{1,0:T(8,128)(2,1)S(1)} %collective-permute-done.8), channel_id=1, source_target_pairs={{4,0},{5,1},{6,2},{7,3},{20,16},{21,17},{22,18},{23,19}} | collective-permute-start | bytes 3145736 | tf_op jit(solution)/shard_map/ppermute | solution.py:23
  224.2 9.5 %collective-permute-done.9 = bf16[2048,256]{1,0:T(8,128)(2,1)S(1)} collective-permute-done((bf16[2048,256]{1,0:T(8,128)(2,1)S(1)}, bf16[2048,256]{1,0:T(8,128)(2,1)S(1)}, u32[]{:S(2)}, u32[]{:S(2)}) %collective-permute-start.9) | collective-permute-done | bytes 1048608 | tf_op jit(solution)/shard_map/ppermute | solution.py:23
  236.3 2.5 bitcast_dynamic-update-slice_fusion.3
  238.8 24.8 %negate_convert_fusion = bf16[512,2048]{1,0:T(8,128)(2,1)} fusion(bf16[8192,512]{1,0:T(8,128)(2,1)} %bitcast.9, bf16[2048,8192]{1,0:T(8,128)(2,1)} %all-gather.2.cloned.1.call-done), kind=kOutput, calls=%fused_computation.4 | convolution fusion | flops 17181966336 | bytes 44040192 | tf_op jit(solution)/shard_map/dot_general | solution.py:67
  263.6 6.2 %copy.32 = bf16[2048,2,256]{2,1,0:T(2,128)(2,1)} copy(bf16[2048,2,256]{0,2,1:T(8,128)(2,1)} %bitcast.121) | data formatting | bytes 4194304 | tf_op jit(solution)/shard_map/reshape | solution.py:69
  276.1 2.5 collective-permute-start.12
  278.6 9.6 %fusion.11 = f32[1024,256]{0,1:T(8,128)S(1)} fusion(bf16[8192,256]{1,0:T(8,128)(2,1)} %bitcast.15, bf16[2048,8192]{1,0:T(8,128)(2,1)} %all-gather.2.cloned.1.call-done), kind=kOutput, calls=%fused_computation.21 | convolution fusion | flops 4294967296 | bytes 22020096 | tf_op jit(solution)/shard_map/dot_general | solution.py:89
  288.3 12.9 %fusion = f32[256,1024]{1,0:T(8,128)} fusion(bf16[8192,256]{1,0:T(8,128)(2,1)} %bitcast.15, bf16[2048,8192]{1,0:T(8,128)(2,1)} %all-gather.2.cloned.1.call-done), kind=kOutput, calls=%fused_computation | convolution fusion | flops 4294967296 | bytes 22020096 | tf_op jit(solution)/shard_map/dot_general | solution.py:92
  303.4 8.8 %collective-permute-start.13 = (f32[3,256,256]{2,1,0:T(8,128)}, f32[3,256,256]{2,1,0:T(8,128)}, u32[]{:S(2)}, u32[]{:S(2)}) collective-permute-start(f32[3,256,256]{2,1,0:T(8,128)} %fusion.36), channel_id=1, source_target_pairs={{0,12},{4,8},{8,4},{12,0},{1,13},{5,9},{9,5},{13,1},{2,14},{6,10},... | collective-permute-start | bytes 2359304 | tf_op jit(solution)/shard_map/ppermute | solution.py:10
  312.2 3.1 fusion.6
  315.3 2.7 convolution_bitcast_fusion.3
  320.6 2.5 copy.27
  324.4 7.5 %collective-permute-done.14 = f32[1,256,256]{2,1,0:T(8,128)} collective-permute-done((f32[1,256,256]{2,1,0:T(8,128)}, f32[1,256,256]{2,1,0:T(8,128)}, u32[]{:S(2)}, u32[]{:S(2)}) %collective-permute-start.14) | collective-permute-done | bytes 262176 | tf_op jit(solution)/shard_map/ppermute | solution.py:10
  333.5 14.3 %collective-permute-done.13 = f32[3,256,256]{2,1,0:T(8,128)} collective-permute-done((f32[3,256,256]{2,1,0:T(8,128)}, f32[3,256,256]{2,1,0:T(8,128)}, u32[]{:S(2)}, u32[]{:S(2)}) %collective-permute-start.13) | collective-permute-done | bytes 786464 | tf_op jit(solution)/shard_map/ppermute | solution.py:10
  (86 shorter events, 49.5 us)
Async XLA Ops:
  7.2 231.6 %all-gather.2.cloned.1.call-start = ((), (), s32[]{:S(2)}) async-start(), calls=%async_computation | async-start | bytes 41943040 | tf_op jit(solution)/shard_map/all_gather | solution.py:61
  11.4 110.9 %copy-start.14 = (bf16[1,256,256]{2,1,0:T(8,128)(2,1)S(1)}, bf16[1,256,256]{2,1,0:T(8,128)(2,1)}, u32[]{:S(2)}) copy-start(bf16[1,256,256]{2,1,0:T(8,128)(2,1)} %param.16) | copy-start | bytes 393220
  13.9 49.5 %collective-permute-start = (bf16[2048,512]{1,0:T(8,128)(2,1)}, bf16[2048,512]{1,0:T(8,128)(2,1)S(1)}, u32[]{:S(2)}, u32[]{:S(2)}) collective-permute-start(bf16[2048,512]{1,0:T(8,128)(2,1)} %copy.23), channel_id=1, source_target_pairs={{0,4},{4,8},{8,12},{1,5},{5,9},{9,13},{2,6},{6,10},{10,14},{3,7},{... | collective-permute-start | bytes 6291464 | tf_op jit(solution)/shard_map/ppermute | solution.py:22
  17.4 50.8 %collective-permute-start.3 = (bf16[2048,512]{1,0:T(8,128)(2,1)}, bf16[2048,512]{1,0:T(8,128)(2,1)S(1)}, u32[]{:S(2)}, u32[]{:S(2)}) collective-permute-start(bf16[2048,512]{1,0:T(8,128)(2,1)} %copy.23), channel_id=1, source_target_pairs={{4,0},{8,4},{12,8},{5,1},{9,5},{13,9},{6,2},{10,6},{14,10},{7,3},{... | collective-permute-start | bytes 6291464 | tf_op jit(solution)/shard_map/ppermute | solution.py:23
  63.3 54.5 %copy-start.11 = (bf16[2048,512]{1,0:T(8,128)(2,1)}, bf16[2048,512]{1,0:T(8,128)(2,1)S(1)}, u32[]{:S(2)}) copy-start(bf16[2048,512]{1,0:T(8,128)(2,1)S(1)} %collective-permute-done) | copy-start | bytes 6291460
  63.3 47.6 %collective-permute-start.1 = (bf16[2048,512]{1,0:T(8,128)(2,1)S(1)}, bf16[2048,512]{1,0:T(8,128)(2,1)}, u32[]{:S(2)}, u32[]{:S(2)}) collective-permute-start(bf16[2048,512]{1,0:T(8,128)(2,1)S(1)} %collective-permute-done), channel_id=1, source_target_pairs={{4,8},{8,12},{5,9},{9,13},{6,10},{10,14},{7,11},{11,15},{20,24},{2... | collective-permute-start | bytes 6291464 | tf_op jit(solution)/shard_map/ppermute | solution.py:22
  69.5 48.3 %collective-permute-start.4 = (bf16[2048,512]{1,0:T(8,128)(2,1)S(1)}, bf16[2048,512]{1,0:T(8,128)(2,1)}, u32[]{:S(2)}, u32[]{:S(2)}) collective-permute-start(bf16[2048,512]{1,0:T(8,128)(2,1)S(1)} %collective-permute-done.3), channel_id=1, source_target_pairs={{4,0},{8,4},{5,1},{9,5},{6,2},{10,6},{7,3},{11,7},{20,16},{24,20},... | collective-permute-start | bytes 6291464 | tf_op jit(solution)/shard_map/ppermute | solution.py:23
  110.9 13.0 %collective-permute-start.2 = (bf16[2048,512]{1,0:T(8,128)(2,1)}, bf16[2048,512]{1,0:T(8,128)(2,1)}, u32[]{:S(2)}, u32[]{:S(2)}) collective-permute-start(bf16[2048,512]{1,0:T(8,128)(2,1)} %collective-permute-done.1), channel_id=1, source_target_pairs={{8,12},{9,13},{10,14},{11,15},{24,28},{25,29},{26,30},{27,31}} | collective-permute-start | bytes 6291464 | tf_op jit(solution)/shard_map/ppermute | solution.py:22
  117.9 45.7 %collective-permute-start.5 = (bf16[2048,512]{1,0:T(8,128)(2,1)}, bf16[2048,512]{1,0:T(8,128)(2,1)}, u32[]{:S(2)}, u32[]{:S(2)}) collective-permute-start(bf16[2048,512]{1,0:T(8,128)(2,1)} %collective-permute-done.4), channel_id=1, source_target_pairs={{4,0},{5,1},{6,2},{7,3},{20,16},{21,17},{22,18},{23,19}} | collective-permute-start | bytes 6291464 | tf_op jit(solution)/shard_map/ppermute | solution.py:23
  163.5 24.3 %collective-permute-start.7 = (bf16[2048,256]{1,0:T(8,128)(2,1)S(1)}, bf16[2048,256]{1,0:T(8,128)(2,1)}, u32[]{:S(2)}, u32[]{:S(2)}) collective-permute-start(bf16[2048,256]{1,0:T(8,128)(2,1)S(1)} %convolution_convert_fusion.1), channel_id=1, source_target_pairs={{4,0},{8,4},{12,8},{5,1},{9,5},{13,9},{6,2},{10,6},{14,10},{7,3},{... | collective-permute-start | bytes 3145736 | tf_op jit(solution)/shard_map/ppermute | solution.py:23
  167.9 2.5 copy-start.19
  172.9 3.9 %copy-start.2 = (bf16[1,2048,512]{2,1,0:T(8,128)(2,1)S(1)}, bf16[1,2048,512]{2,1,0:T(8,128)(2,1)}, u32[]{:S(2)}) copy-start(bf16[1,2048,512]{2,1,0:T(8,128)(2,1)} %copy.22) | copy-start | bytes 6291460
  176.8 15.4 %copy-start.12 = (bf16[2048,512]{1,0:T(8,128)(2,1)S(1)}, bf16[2048,512]{1,0:T(8,128)(2,1)}, u32[]{:S(2)}) copy-start(bf16[2048,512]{1,0:T(8,128)(2,1)} %copy-done.11) | copy-start | bytes 6291460
  178.3 23.9 %collective-permute-start.6 = (bf16[2048,256]{1,0:T(8,128)(2,1)S(1)}, bf16[2048,256]{1,0:T(8,128)(2,1)S(1)}, u32[]{:S(2)}, u32[]{:S(2)}) collective-permute-start(bf16[2048,256]{1,0:T(8,128)(2,1)S(1)} %convolution_convert_fusion.1), channel_id=1, source_target_pairs={{0,4},{4,8},{8,12},{1,5},{5,9},{9,13},{2,6},{6,10},{10,14},{3,7},{... | collective-permute-start | bytes 3145736 | tf_op jit(solution)/shard_map/ppermute | solution.py:22
  187.8 23.6 %collective-permute-start.8 = (bf16[2048,256]{1,0:T(8,128)(2,1)}, bf16[2048,256]{1,0:T(8,128)(2,1)S(1)}, u32[]{:S(2)}, u32[]{:S(2)}) collective-permute-start(bf16[2048,256]{1,0:T(8,128)(2,1)} %collective-permute-done.7), channel_id=1, source_target_pairs={{4,0},{8,4},{5,1},{9,5},{6,2},{10,6},{7,3},{11,7},{20,16},{24,20},... | collective-permute-start | bytes 3145736 | tf_op jit(solution)/shard_map/ppermute | solution.py:23
  202.2 21.2 %collective-permute-start.10 = (bf16[2048,256]{1,0:T(8,128)(2,1)S(1)}, bf16[2048,256]{1,0:T(8,128)(2,1)S(1)}, u32[]{:S(2)}, u32[]{:S(2)}) collective-permute-start(bf16[2048,256]{1,0:T(8,128)(2,1)S(1)} %collective-permute-done.6), channel_id=1, source_target_pairs={{4,8},{8,12},{5,9},{9,13},{6,10},{10,14},{7,11},{11,15},{20,24},{2... | collective-permute-start | bytes 3145736 | tf_op jit(solution)/shard_map/ppermute | solution.py:22
  211.4 22.4 %collective-permute-start.9 = (bf16[2048,256]{1,0:T(8,128)(2,1)S(1)}, bf16[2048,256]{1,0:T(8,128)(2,1)S(1)}, u32[]{:S(2)}, u32[]{:S(2)}) collective-permute-start(bf16[2048,256]{1,0:T(8,128)(2,1)S(1)} %collective-permute-done.8), channel_id=1, source_target_pairs={{4,0},{5,1},{6,2},{7,3},{20,16},{21,17},{22,18},{23,19}} | collective-permute-start | bytes 3145736 | tf_op jit(solution)/shard_map/ppermute | solution.py:23
  223.3 13.0 %collective-permute-start.11 = (bf16[2048,256]{1,0:T(8,128)(2,1)S(1)}, bf16[2048,256]{1,0:T(8,128)(2,1)S(1)}, u32[]{:S(2)}, u32[]{:S(2)}) collective-permute-start(bf16[2048,256]{1,0:T(8,128)(2,1)S(1)} %collective-permute-done.10), channel_id=1, source_target_pairs={{8,12},{9,13},{10,14},{11,15},{24,28},{25,29},{26,30},{27,31}} | collective-permute-start | bytes 3145736 | tf_op jit(solution)/shard_map/ppermute | solution.py:22
  272.2 2.9 copy-start.3
  274.6 4.0 %copy-start.8 = (bf16[1,2048,256]{2,0,1:T(2,128)(2,1)}, bf16[1,2048,256]{2,0,1:T(2,128)(2,1)S(1)}, u32[]{:S(2)}) copy-start(bf16[1,2048,256]{2,0,1:T(2,128)(2,1)S(1)} %fusion.30) | copy-start | bytes 3145732
  276.1 25.1 %collective-permute-start.12 = (f32[3,256,256]{2,1,0:T(8,128)}, f32[3,256,256]{2,1,0:T(8,128)}, u32[]{:S(2)}, u32[]{:S(2)}) collective-permute-start(f32[3,256,256]{2,1,0:T(8,128)} %pad_maximum_fusion), channel_id=1, source_target_pairs={{0,4},{4,0},{8,12},{12,8},{1,5},{5,1},{9,13},{13,9},{2,6},{6,2},{1... | collective-permute-start | bytes 2359304 | tf_op jit(solution)/shard_map/ppermute | solution.py:10
  288.2 24.0 %copy-start.6 = (f32[1024,256]{0,1:T(8,128)}, f32[1024,256]{0,1:T(8,128)S(1)}, u32[]{:S(2)}) copy-start(f32[1024,256]{0,1:T(8,128)S(1)} %fusion.11) | copy-start | bytes 3145732
  288.2 13.0 %copy-start.4 = (f32[2,256,256]{2,1,0:T(8,128)S(1)}, f32[2,256,256]{2,1,0:T(8,128)}, u32[]{:S(2)}) copy-start(f32[2,256,256]{2,1,0:T(8,128)} %copy-done.3) | copy-start | bytes 1572868
  301.2 11.0 %copy-start.7 = (f32[256,1024]{1,0:T(8,128)S(1)}, f32[256,1024]{1,0:T(8,128)}, u32[]{:S(2)}) copy-start(f32[256,1024]{1,0:T(8,128)} %fusion) | copy-start | bytes 3145732
  303.4 44.4 %collective-permute-start.13 = (f32[3,256,256]{2,1,0:T(8,128)}, f32[3,256,256]{2,1,0:T(8,128)}, u32[]{:S(2)}, u32[]{:S(2)}) collective-permute-start(f32[3,256,256]{2,1,0:T(8,128)} %fusion.36), channel_id=1, source_target_pairs={{0,12},{4,8},{8,4},{12,0},{1,13},{5,9},{9,5},{13,1},{2,14},{6,10},... | collective-permute-start | bytes 2359304 | tf_op jit(solution)/shard_map/ppermute | solution.py:10
  315.3 4.4 %copy-start.15 = (bf16[1,256,256]{2,1,0:T(8,128)(2,1)S(1)}, bf16[1,256,256]{2,1,0:T(8,128)(2,1)}, u32[]{:S(2)}) copy-start(bf16[1,256,256]{2,1,0:T(8,128)(2,1)} %param.16) | copy-start | bytes 393220
  315.3 5.3 %copy-start.1 = (bf16[512,2048]{1,0:T(8,128)(2,1)S(1)}, bf16[512,2048]{1,0:T(8,128)(2,1)}, u32[]{:S(2)}) copy-start(bf16[512,2048]{1,0:T(8,128)(2,1)} %negate_convert_fusion) | copy-start | bytes 6291460
  318.0 13.9 %collective-permute-start.14 = (f32[1,256,256]{2,1,0:T(8,128)}, f32[1,256,256]{2,1,0:T(8,128)}, u32[]{:S(2)}, u32[]{:S(2)}) collective-permute-start(f32[1,256,256]{2,1,0:T(8,128)} %convolution_bitcast_fusion.3), channel_id=1, source_target_pairs={{0,4},{4,0},{8,12},{12,8},{1,5},{5,1},{9,13},{13,9},{2,6},{6,2},{1... | collective-permute-start | bytes 786440 | tf_op jit(solution)/shard_map/ppermute | solution.py:10
  333.0 19.8 %collective-permute-start.15 = (f32[1,256,256]{2,1,0:T(8,128)S(1)}, f32[1,256,256]{2,1,0:T(8,128)S(1)}, u32[]{:S(2)}, u32[]{:S(2)}) collective-permute-start(f32[1,256,256]{2,1,0:T(8,128)S(1)} %add.87), channel_id=1, source_target_pairs={{0,12},{4,8},{8,4},{12,0},{1,13},{5,9},{9,5},{13,1},{2,14},{6,10},... | collective-permute-start | bytes 786440 | tf_op jit(solution)/shard_map/ppermute | solution.py:10
  349.3 3.5 copy-start.16
  349.6 3.9 %copy-start.18 = (bf16[2,256,256]{2,1,0:T(8,128)(2,1)}, bf16[2,256,256]{2,1,0:T(8,128)(2,1)S(1)}, u32[]{:S(2)}) copy-start(bf16[2,256,256]{2,1,0:T(8,128)(2,1)S(1)} %fusion.18) | copy-start | bytes 786436
  350.2 3.3 copy-start.17
  (5 other events, 9.9 us)
Sparse Core Ops, SparseCore 0:
  9.6 202.6 all-gather.1
